TPU v7x, 256 devices: a whole 4x4x8 slice. The times are simulated.
256 devices in a mesh: sample: 8 (over y, core), slab: 32 (over x, z).
Axes of the slice: x: 4, y: 4, z: 8, core: 2. Of those that a mesh axis runs over, the one named last changes fastest.
Arguments:
- volume: bfloat16 [8, 32, 32, 32, 128], P('sample', 'slab'), may hold values from -6 to 6
- kernel: bfloat16 [27, 128, 128], replicated, may hold values from -0.109375 to 0.109375
- cotangent: bfloat16 [8, 32, 32, 32, 128], P('sample', 'slab'), may hold values from -6 to 6
Outputs:
- response: bfloat16 [8, 32, 32, 32, 128], P('sample', 'slab')
- grad_volume: bfloat16 [8, 32, 32, 32, 128], P('sample', 'slab')
- grad_kernel: float32 [128, 27, 128], P('slab')
All inputs are finite; a program needn't handle non-finite values.
Results may differ from a plain program's by a relative error of at most 0.001.
Values may be sent and summed in bfloat16 or wider, within the bound.
No kernel may reach another device: no remote copies, remote signals or barrier semaphores. Data moves between devices by JAX's collectives and lax.ppermute only.
A program may use at most 64 MiB of HBM per device.

v0:
```python
import math

import jax
import jax.numpy as jnp
from jax import lax
from jax.sharding import PartitionSpec as P


def extended(shard, sides, width):
    for axis, dim in sides:
        peers, length = (lax.axis_size(axis), shard.shape[dim])
        up = [(i, (i + 1) % peers) for i in range(peers - 1)]
        down = [(j, i) for i, j in up]
        last = lax.slice_in_dim(shard, length - width, length, axis=dim)
        initial = lax.slice_in_dim(shard, 0, width, axis=dim)
        before = lax.ppermute(last, axis, up)
        after = lax.ppermute(initial, axis, down)
        shard = jnp.concatenate([before, shard, after], axis=dim)
    return shard


def pad_sides(field):
    return jnp.pad(field, ((0, 0), (0, 0), (1, 1), (1, 1), (0, 0)))


def window_of(padded, start_z, start_y, start_x, planes, grid_rows, grid_cols):
    return padded[
        :, start_z : start_z + planes, start_y : start_y + grid_rows, start_x : start_x + grid_cols
    ]


def on_device(volume, kernel, cotangent):
    local_batch, planes, grid_rows, grid_cols, channels = volume.shape
    factor = 1.0 / math.sqrt(
        local_batch
        * lax.axis_size("sample")
        * planes
        * lax.axis_size("slab")
        * grid_rows
        * grid_cols
    )
    padded = pad_sides(extended(volume, (("slab", 1),), 1))
    flat_up = cotangent.reshape(-1, channels)
    output = jnp.zeros((flat_up.shape[0], channels), jnp.float32)
    kernel_terms = []
    for tap_index in range(27):
        along_z = tap_index // 9
        along_y = tap_index // 3 % 3
        along_x = tap_index % 3
        window = window_of(padded, along_z, along_y, along_x, planes, grid_rows, grid_cols).reshape(
            -1, channels
        )
        output = output + jnp.dot(window, kernel[tap_index], preferred_element_type=jnp.float32)
        kernel_terms.append(jnp.dot(flat_up.T, window, preferred_element_type=jnp.float32))
    response = output.reshape(volume.shape).astype(jnp.bfloat16)
    shape_full = volume.shape
    padded_up = pad_sides(extended(cotangent, (("slab", 1),), 1))
    backward = jnp.zeros((flat_up.shape[0], channels), jnp.float32)
    for tap_index in range(27):
        along_z = tap_index // 9
        along_y = tap_index // 3 % 3
        along_x = tap_index % 3
        mirror = window_of(
            padded_up, 2 - along_z, 2 - along_y, 2 - along_x, planes, grid_rows, grid_cols
        ).reshape(-1, channels)
        backward = backward + jnp.dot(
            mirror, kernel[tap_index].T, preferred_element_type=jnp.float32
        )
    grad_volume = backward.reshape(shape_full).astype(jnp.bfloat16)
    local_grad = jnp.stack(kernel_terms, 1) * factor
    over_samples = lax.psum(local_grad, "sample")
    grad_kernel = lax.psum_scatter(over_samples, "slab", scatter_dimension=0, tiled=True)
    return (response, grad_volume, grad_kernel)


def solution(mesh):
    return jax.shard_map(
        on_device,
        mesh=mesh,
        in_specs=(
            P("sample", "slab", None, None, None),
            P(),
            P("sample", "slab", None, None, None),
        ),
        out_specs=(
            P("sample", "slab", None, None, None),
            P("sample", "slab", None, None, None),
            P("slab", None, None),
        ),
        check_vma=False,
    )
```

profile of v0, /device:TPU:1, one launch (start us, length us, event | category | flops | bytes accessed | tf_op | source)
XLA Modules:
  0.0 291.4 jit_solution(5189730536325530757)
XLA Ops:
  7.2 4.4 %collective-permute-start.2 = (bf16[1,1,32,32,128]{4,3,2,1,0:T(8,128)(2,1)}, bf16[1,1,32,32,128]{4,3,2,1,0:T(8,128)(2,1)S(1)}, u32[]{:S(2)}, u32[]{:S(2)}) collective-permute-start(bf16[1,1,32,32,128]{4,3,2,1,0:T(8,128)(2,1)} %param.5), channel_id=1, source_target_pairs={{0,1},{1,2},{2,3},{3,4},{4,5},{5,6},{6,7},{7,8},{8,9},{9,10},{10,1... | collective-permute-start | bytes 786440 | tf_op jit(solution)/shard_map/ppermute | solution.py:16
  11.6 1.3 collective-permute-start.3
  12.9 4.2 %collective-permute-start = (bf16[1,1,32,32,128]{4,3,2,1,0:T(8,128)(2,1)}, bf16[1,1,32,32,128]{4,3,2,1,0:T(8,128)(2,1)S(1)}, u32[]{:S(2)}, u32[]{:S(2)}) collective-permute-start(bf16[1,1,32,32,128]{4,3,2,1,0:T(8,128)(2,1)} %param.3), channel_id=1, source_target_pairs={{0,1},{1,2},{2,3},{3,4},{4,5},{5,6},{6,7},{7,8},{8,9},{9,10},{10,1... | collective-permute-start | bytes 786440 | tf_op jit(solution)/shard_map/ppermute | solution.py:16
  17.1 1.3 collective-permute-start.1
  18.4 2.5 collective-permute-done.3
  20.9 1.5 select_maximum_fusion
  22.4 2.4 fusion.229
  24.9 1.1 fusion.230
  26.0 0.3 collective-permute-done.1
  26.3 0.4 select_maximum_fusion.2
  27.0 1.2 fusion.232
  28.2 2.4 fusion.231
  30.8 0.3 fusion.33
  31.1 0.3 fusion.32
  31.4 0.3 fusion.31
  31.7 0.3 fusion.30
  31.9 0.3 fusion.29
  32.8 0.3 fusion.26
  33.9 0.3 fusion.22
  34.5 0.3 fusion.20
  35.3 0.3 fusion.17
  36.4 0.3 fusion.13
  37.0 0.3 fusion.11
  38.0 2.5 copy.13
  40.5 1.1 copy-done.1
  49.8 0.4 copy-done.29
  50.8 0.9 fusion.8
  52.6 0.5 copy-done.30
  59.7 0.9 fusion.7
  60.6 196.1 %reduce-scatter.2.cloned.1.call-done = f32[4,27,128]{2,1,0:T(8,128)} async-done(((f32[128,27,128]{2,1,0:T(8,128)}), f32[4,27,128]{2,1,0:T(8,128)}) %reduce-scatter.2.cloned.1.call-update) | async-done | bytes 55312 | tf_op jit(solution)/shard_map/reduce_scatter | solution.py:72
  256.7 27.3 %psum.8 = f32[4,27,128]{2,1,0:T(8,128)S(1)} all-reduce(f32[4,27,128]{2,1,0:T(8,128)} %reduce-scatter.2.cloned.1.call-done), channel_id=1, replica_groups=mesh['sample'=8,'slab'=32] {'sample'}, use_global_device_ids=true, to_apply=%region_0.1 | all-reduce | flops 13824 | bytes 110592 | tf_op jit(solution)/shard_map/psum | solution.py:71
  283.9 0.7 copy.14
  (174 shorter events, 20.2 us)
Async XLA Ops:
  7.2 249.5 %reduce-scatter.2.cloned.1.call-start = ((), (), s32[]{:S(2)}) async-start(), calls=%async_computation.1 | async-start | bytes 2162688 | tf_op jit(solution)/shard_map/reduce_scatter | solution.py:72
  7.2 11.2 %collective-permute-start.2 = (bf16[1,1,32,32,128]{4,3,2,1,0:T(8,128)(2,1)}, bf16[1,1,32,32,128]{4,3,2,1,0:T(8,128)(2,1)S(1)}, u32[]{:S(2)}, u32[]{:S(2)}) collective-permute-start(bf16[1,1,32,32,128]{4,3,2,1,0:T(8,128)(2,1)} %param.5), channel_id=1, source_target_pairs={{0,1},{1,2},{2,3},{3,4},{4,5},{5,6},{6,7},{7,8},{8,9},{9,10},{10,1... | collective-permute-start | bytes 786440 | tf_op jit(solution)/shard_map/ppermute | solution.py:16
  11.6 9.3 %collective-permute-start.3 = (bf16[1,1,32,32,128]{4,3,2,1,0:T(8,128)(2,1)}, bf16[1,1,32,32,128]{4,3,2,1,0:T(8,128)(2,1)S(1)}, u32[]{:S(2)}, u32[]{:S(2)}) collective-permute-start(bf16[1,1,32,32,128]{4,3,2,1,0:T(8,128)(2,1)} %param.5), channel_id=1, source_target_pairs={{1,0},{2,1},{3,2},{4,3},{5,4},{6,5},{7,6},{8,7},{9,8},{10,9},{11,1... | collective-permute-start | bytes 786440 | tf_op jit(solution)/shard_map/ppermute | solution.py:17
  12.9 13.1 %collective-permute-start = (bf16[1,1,32,32,128]{4,3,2,1,0:T(8,128)(2,1)}, bf16[1,1,32,32,128]{4,3,2,1,0:T(8,128)(2,1)S(1)}, u32[]{:S(2)}, u32[]{:S(2)}) collective-permute-start(bf16[1,1,32,32,128]{4,3,2,1,0:T(8,128)(2,1)} %param.3), channel_id=1, source_target_pairs={{0,1},{1,2},{2,3},{3,4},{4,5},{5,6},{6,7},{7,8},{8,9},{9,10},{10,1... | collective-permute-start | bytes 786440 | tf_op jit(solution)/shard_map/ppermute | solution.py:16
  17.1 9.2 %collective-permute-start.1 = (bf16[1,1,32,32,128]{4,3,2,1,0:T(8,128)(2,1)}, bf16[1,1,32,32,128]{4,3,2,1,0:T(8,128)(2,1)S(1)}, u32[]{:S(2)}, u32[]{:S(2)}) collective-permute-start(bf16[1,1,32,32,128]{4,3,2,1,0:T(8,128)(2,1)} %param.3), channel_id=1, source_target_pairs={{1,0},{2,1},{3,2},{4,3},{5,4},{6,5},{7,6},{8,7},{9,8},{10,9},{11,1... | collective-permute-start | bytes 786440 | tf_op jit(solution)/shard_map/ppermute | solution.py:17
  20.9 1.5 copy-start.3
  24.9 1.4 copy-start.2
  24.9 1.8 copy-start
  40.5 1.2 copy-start.1
  40.5 1.2 copy-start.7
  40.5 1.4 copy-start.6
  40.5 1.7 copy-start.5
  40.5 1.9 copy-start.9
  40.5 2.1 copy-start.8
  42.6 1.0 copy-start.49
  42.9 1.0 copy-start.4
  43.4 1.0 copy-start.48
  44.1 1.0 copy-start.46
  44.3 1.0 copy-start.45
  45.1 1.0 copy-start.43
  46.6 1.0 copy-start.39
  48.3 1.0 copy-start.31
  49.8 1.0 copy-start.25
  50.2 1.5 copy-start.36
  50.5 1.4 copy-start.34
  50.8 1.4 copy-start.32
  52.6 1.0 copy-start.26
  55.5 1.0 copy-start.18
  56.5 1.0 copy-start.15
  56.8 1.0 copy-start.14
  57.2 1.0 copy-start.13
  58.7 1.0 copy-start.10
  (25 other events, 24.5 us)
Sparse Core Ops, SparseCore 0:
  40.6 216.0 reduce-scatter.1
where the time goes:
time: 293 us; the launch traced here: 291 us
  waiting for transfers between devices  199 us (68%)
  blocking collectives  27.3 us (9%)
  matrix products  20.5 us (7%)
  local copies, waits for them, and re-layouts  16.7 us (6%)
  between operations  14.9 us (5%)
  starting transfers between devices  11.2 us (4%)
    reduce_scatter x1, waiting for transfers between devices, on_device(): lax.psum_scatter(over_samples, 'slab', scatter_dimension=0, tiled=True)  196 us
    psum x1, blocking collectives, on_device(): over_samples = lax.psum(local_grad, 'sample')  27.3 us
    ppermute x2, starting transfers between devices, extended(): before = lax.ppermute(last, axis, up)  8.57 us
    dot_general x27, matrix products, on_device(): jnp.dot(flat_up.T, window, preferred_element_type=jnp.float32)  7.37 us
    slice x4, local copies, waits for them, and re-layouts, window_of(): padded[:, start_z:start_z + planes, start_y:start_y + grid_rows, start_x:...  7.13 us
    unnamed x105, local copies, waits for them, and re-layouts  7.07 us
    dot_general x27, matrix products, on_device(): jnp.dot(mirror, kernel[tap_index].T, preferred_element_type=jnp.float32)  6.76 us
    dot_general x27, matrix products, on_device(): jnp.dot(window, kernel[tap_index], preferred_element_type=jnp.float32)  6.33 us
  transfers between devices with their start and end apart: 5, of which 3 were waited for; matrix products, arithmetic and copies ran while one was open for 6% of the time, Pallas kernels for 0%

commit v1 on v0

v1 whole, which is shorter than its diff:
```python
import functools
import math

import jax
import jax.numpy as jnp
from jax import lax
from jax.experimental import pallas as pl
from jax.experimental.pallas import tpu as pltpu
from jax.sharding import PartitionSpec as P

AXES = ("sample", "slab")
YS, CORES, XS, ZS = 4, 2, 4, 8
GRID, CELLS, C = 32, 1024, 128
PADDED = CELLS + 2 * GRID
F32, BF16 = jnp.float32, jnp.bfloat16
ANY = pl.BlockSpec(memory_space=pl.ANY)
VMEM = pl.BlockSpec(memory_space=pltpu.VMEM)
SMEM = pl.BlockSpec(memory_space=pltpu.SMEM)


def move(array, target):
    perm = []
    for y in range(YS):
        for core in range(CORES):
            for slab in range(XS * ZS):
                to = target(y, core, slab)
                if to is not None:
                    ty, tcore, tslab = to
                    perm.append(
                        ((y * CORES + core) * XS * ZS + slab, (ty * CORES + tcore) * XS * ZS + tslab)
                    )
    return lax.ppermute(array, AXES, perm)


def partner(y, core, slab):
    return y, core, slab ^ 1


def other(y, core, slab):
    to = slab - 1 if slab % 2 == 0 else slab + 1
    return (y, core, to) if 0 <= to < XS * ZS else None


def across_x(s):
    return lambda y, core, slab: (y, core, slab ^ (s * ZS))


def across_z(t):
    return lambda y, core, slab: (y, core, slab ^ (2 * t))


def across_y(s):
    return lambda y, core, slab: (y ^ s, core, slab)


def zero_edges(padded):
    padded[0:GRID] = jnp.zeros((GRID, C), BF16)
    padded[GRID + CELLS : PADDED] = jnp.zeros((GRID, C), BF16)


def row_order(place):
    r = lax.broadcasted_iota(jnp.int32, (C, C), 0)
    o = lax.broadcasted_iota(jnp.int32, (C, C), 1)
    half, s, t, j = r >> 6, (r >> 4) & 3, (r >> 2) & 3, r & 3
    wanted = ((place[1] ^ s) << 5) + ((place[2] ^ t) << 3) + ((place[0] ^ half) << 2) + j
    return jnp.where(o == wanted, 1.0, 0.0).astype(BF16)


def fill_rows(rows, order, cot):
    k = lax.broadcasted_iota(jnp.int32, (256, 256), 0)
    n = lax.broadcasted_iota(jnp.int32, (256, 256), 1)
    same = (k >> 5) == (n >> 5)
    left = jnp.where(same & (k == n + 1), 1.0, 0.0).astype(BF16)
    right = jnp.where(same & (k == n - 1), 1.0, 0.0).astype(BF16)
    for block in range(0, CELLS, 256):
        cells = slice(block, block + 256)
        turned = lax.dot_general(
            order, cot[cells], (((1,), (1,)), ((), ())), preferred_element_type=F32
        ).astype(BF16)
        rows[0:C, cells] = jnp.dot(turned, left, preferred_element_type=F32).astype(BF16)
        rows[C : 2 * C, cells] = turned
        rows[2 * C : 3 * C, cells] = jnp.dot(turned, right, preferred_element_type=F32).astype(BF16)


def product(rows, padded):
    wide = jnp.concatenate([padded[b * GRID : b * GRID + CELLS] for b in range(3)], axis=1)
    return jnp.dot(rows[...], wide, preferred_element_type=F32)


def write_pieces(total, keep, send):
    for s in range(4):
        for c in range(3):
            start = c * C + s * 16
            keep[s, c] = total[start : start + 16]
            send[s, c] = total[start + 64 : start + 80]


def centre_kernel(place, vol, cot, keep, send, padded, cots, rows, sems):
    copies = [
        pltpu.make_async_copy(cot, cots, sems.at[0]),
        pltpu.make_async_copy(vol, padded.at[pl.ds(GRID, CELLS)], sems.at[1]),
    ]
    for copy in copies:
        copy.start()
    zero_edges(padded)
    order = row_order(place)
    copies[0].wait()
    fill_rows(rows, order, cots)
    copies[1].wait()
    write_pieces(product(rows, padded), keep, send)


def side_kernel(place, vol, cot, near_vol, near_cot, keep, send, padded, cots, rows, sems):
    copies = [
        pltpu.make_async_copy(cot, cots.at[0], sems.at[0]),
        pltpu.make_async_copy(near_cot, cots.at[1], sems.at[1]),
        pltpu.make_async_copy(near_vol, padded.at[0, pl.ds(GRID, CELLS)], sems.at[2]),
        pltpu.make_async_copy(vol, padded.at[1, pl.ds(GRID, CELLS)], sems.at[3]),
    ]
    for copy in copies:
        copy.start()
    zero_edges(padded.at[0])
    zero_edges(padded.at[1])
    order = row_order(place)
    copies[0].wait()
    fill_rows(rows.at[0], order, cots.at[0])
    copies[1].wait()
    fill_rows(rows.at[1], order, cots.at[1])
    copies[2].wait()
    copies[3].wait()
    total = product(rows.at[0], padded.at[0]) + product(rows.at[1], padded.at[1])
    write_pieces(total, keep, send)


def conv_kernel(backward, weights, before, own, after, out, padded, weight, sems):
    planes = (after, own, before) if backward else (before, own, after)
    copies = [
        pltpu.make_async_copy(planes[a], padded.at[a, pl.ds(GRID, CELLS)], sems.at[a])
        for a in range(3)
    ] + [pltpu.make_async_copy(weights, weight, sems.at[3])]
    for copy in copies:
        copy.start()
    for a in range(3):
        zero_edges(padded.at[a])
    for copy in copies:
        copy.wait()
    pairs = [(0, 1), (2, 3), (4, 5), (6, 7), (8,)]

    @pl.loop(0, CELLS // 256)
    def _(block):
        start = pl.multiple_of(block * 256, 256)
        total = jnp.zeros((256, 3 * C), F32)
        for pair in pairs:
            left, right = [], []
            for ab in pair:
                a, b = ab // 3, ab % 3
                shift = (2 - b if backward else b) * GRID
                left.append(padded[a, pl.ds(pl.multiple_of(start + shift, GRID), 256), :])
                if backward:
                    right.append(
                        jnp.concatenate([weight[3 * ab + c] for c in range(3)], axis=0)
                    )
                else:
                    right.append(
                        jnp.concatenate([weight[3 * ab + c] for c in range(3)], axis=1)
                    )
            lhs = jnp.concatenate(left, axis=1)
            rhs = jnp.concatenate(right, axis=1 if backward else 0)
            dims = (((1,), (1 if backward else 0,)), ((), ()))
            total = total + lax.dot_general(lhs, rhs, dims, preferred_element_type=F32)
        low, mid, high = total[:, :C], total[:, C : 2 * C], total[:, 2 * C :]
        if backward:
            low, high = high, low
        x = lax.broadcasted_iota(jnp.int32, (256, C), 0) & (GRID - 1)
        low = jnp.where(x == 0, 0.0, pltpu.roll(low, 1, 0))
        high = jnp.where(x == GRID - 1, 0.0, pltpu.roll(high, 255, 0))
        out[pl.ds(start, 256), :] = (mid + low + high).astype(BF16)


PIECES = jax.ShapeDtypeStruct((4, 3, 16, 3 * C), F32)
PARAMS = pltpu.CompilerParams(vmem_limit_bytes=32 * 1024 * 1024)
TERM_FLOPS = 2 * 9 * CELLS * C * C


def centre(place, vol, cot):
    return pl.pallas_call(
        centre_kernel,
        out_shape=(PIECES, PIECES),
        in_specs=[SMEM, ANY, ANY],
        out_specs=(VMEM, VMEM),
        scratch_shapes=[
            pltpu.VMEM((PADDED, C), BF16),
            pltpu.VMEM((CELLS, C), BF16),
            pltpu.VMEM((3 * C, CELLS), BF16),
            pltpu.SemaphoreType.DMA((2,)),
        ],
        compiler_params=PARAMS,
        cost_estimate=pl.CostEstimate(flops=2 * TERM_FLOPS, bytes_accessed=4 << 20, transcendentals=0),
        name="centre",
    )(place, vol, cot)


def side(place, vol, cot, near_vol, near_cot):
    return pl.pallas_call(
        side_kernel,
        out_shape=(PIECES, PIECES),
        in_specs=[SMEM, ANY, ANY, ANY, ANY],
        out_specs=(VMEM, VMEM),
        scratch_shapes=[
            pltpu.VMEM((2, PADDED, C), BF16),
            pltpu.VMEM((2, CELLS, C), BF16),
            pltpu.VMEM((2, 3 * C, CELLS), BF16),
            pltpu.SemaphoreType.DMA((4,)),
        ],
        compiler_params=PARAMS,
        cost_estimate=pl.CostEstimate(flops=4 * TERM_FLOPS, bytes_accessed=8 << 20, transcendentals=0),
        name="side",
    )(place, vol, cot, near_vol, near_cot)


def conv(backward, weights, before, own, after):
    return pl.pallas_call(
        functools.partial(conv_kernel, backward),
        out_shape=jax.ShapeDtypeStruct((CELLS, C), BF16),
        in_specs=[ANY, ANY, ANY, ANY],
        out_specs=VMEM,
        scratch_shapes=[
            pltpu.VMEM((3, PADDED, C), BF16),
            pltpu.VMEM((27, C, C), BF16),
            pltpu.SemaphoreType.DMA((4,)),
        ],
        compiler_params=PARAMS,
        cost_estimate=pl.CostEstimate(flops=6 * TERM_FLOPS, bytes_accessed=8 << 20, transcendentals=0),
        name="grad_volume" if backward else "response",
    )(weights, before, own, after)


def reduce_x(keep, received):
    total = keep + received
    parts = [move(total[s], across_x(s)) for s in range(1, 4)]
    return total[0] + parts[0] + (parts[1] + parts[2])


def on_device(volume, kernel, cotangent):
    sample, slab = lax.axis_index("sample"), lax.axis_index("slab")
    core, z_odd = sample & 1, slab & 1
    place = jnp.stack([core, slab >> 3, (slab >> 1) & 3]).astype(jnp.int32)
    scale = 1.0 / math.sqrt(YS * CORES * XS * ZS * CELLS)
    vol, cot = volume.reshape(CELLS, C), cotangent.reshape(CELLS, C)

    partner_vol = move(vol, partner)
    other_cot = move(cot, other)
    partner_cot = move(cot, partner)
    other_vol = move(vol, other)
    swap = lambda y, c, s: (y, 1 - c, s)

    keep, send = centre(place, vol, cot)
    centre_sum = reduce_x(keep, move(send, swap))
    keep, send = side(place, vol, cot, partner_vol, other_cot)
    side_sum = reduce_x(keep, move(send, swap))

    even = z_odd == 0
    response = conv(
        False, kernel, jnp.where(even, other_vol, partner_vol), vol, jnp.where(even, partner_vol, other_vol)
    )
    grad_volume = conv(
        True, kernel, jnp.where(even, other_cot, partner_cot), cot, jnp.where(even, partner_cot, other_cot)
    )

    both = jnp.stack([centre_sum, side_sum]).reshape(2, 3, 4, 4, 3 * C)
    pieces = [both[:, :, t].reshape(24, 3 * C) for t in range(4)]
    parts = [move(pieces[t], across_z(t)) for t in range(1, 4)]
    total = pieces[0] + parts[0] + (parts[1] + parts[2])
    parts = [move(total, across_y(s)) for s in range(1, 4)]
    total = (total + parts[0]) + (parts[1] + parts[2])

    def first(y, c, s):
        p = s & 1
        return (y, c, s ^ 1) if c != p else (y, 1 - c, s)

    def second(y, c, s):
        return (y, 1 - c, s ^ 1) if c != (s & 1) else None

    one, two = move(total, first), move(total, second)
    same = core == z_odd
    from_even = jnp.where(same, jnp.where(even, total, one), jnp.where(even, one, two))
    from_odd = jnp.where(same, jnp.where(even, one, total), jnp.where(even, two, one))
    from_even, from_odd = from_even.reshape(2, 3, 4, 3, C), from_odd.reshape(2, 3, 4, 3, C)
    taps = jnp.stack([from_odd[1], from_even[0] + from_odd[0], from_even[1]])
    grad_kernel = (taps.transpose(2, 0, 3, 1, 4) * scale).reshape(4, 27, C)
    return (response.reshape(volume.shape), grad_volume.reshape(volume.shape), grad_kernel)


def solution(mesh):
    planes = P("sample", "slab", None, None, None)
    return jax.shard_map(
        on_device,
        mesh=mesh,
        in_specs=(planes, P(), planes),
        out_specs=(planes, planes, P("slab", None, None)),
        check_vma=False,
    )
```

time: 293 us -> 66.4 us (0.23)
  waiting for transfers between devices: 199 us -> 9.96 us
  starting transfers between devices: 11.2 us -> 41 us
  blocking collectives: 27.3 us -> 0 us
  matrix products: 20.5 us -> 0 us
  local copies, waits for them, and re-layouts: 16.7 us -> 1.83 us
  between operations: 14.9 us -> 0.93 us
  Pallas kernels: 0 us -> 12 us
    reduce_scatter x1 -> x0, waiting for transfers between devices: 196 us -> none  [on_device(): lax.psum_scatter(over_samples, 'slab', scatter_dimension=0, tiled=True)]
    ppermute x4 -> x20, starting transfers between devices: 11.2 us -> 41 us  [move(): return lax.ppermute(array, AXES, perm)]
    psum x1 -> x0, blocking collectives: 27.3 us -> none  [on_device(): over_samples = lax.psum(local_grad, 'sample')]
    dot_general x81 -> x0, matrix products: 20.5 us -> none  [the longest x27 7.37 us: on_device(): jnp.dot(flat_up.T, window, preferred_element_type=jnp.float32)]
    pallas_call x0 -> x4, Pallas kernels: none -> 12 us  [the longest x2 6.64 us: conv(): pl.pallas_call(functools.partial(conv_kernel, backward), out_shape=jax.Sh...]
    ppermute x4 -> x20, waiting for transfers between devices: 2.82 us -> 9.96 us  [move(): return lax.ppermute(array, AXES, perm)]
    slice x4 -> x3, local copies, waits for them, and re-layouts: 7.13 us -> 0.04 us  [the longest x2 0.03 us: on_device(): taps = jnp.stack([from_odd[1], from_even[0] + from_odd[0], from_even[1]])]
    unnamed x105 -> x7, local copies, waits for them, and re-layouts: 7.07 us -> 0.97 us
  transfers between devices with their start and end apart: 5 -> 20, of which waited for: 3 -> 6; matrix products, arithmetic and copies ran while one was open for 6% -> 1% of each run, Pallas kernels for 0% -> 15%
where the time goes in v1:
time: 66.4 us; the launch traced here: 66.1 us
  starting transfers between devices  41 us (62%)
  Pallas kernels  12 us (18%)
  waiting for transfers between devices  9.96 us (15%)
  local copies, waits for them, and re-layouts  1.83 us (3%)
  between operations  0.93 us (1%)
    ppermute x20, starting transfers between devices, move(): return lax.ppermute(array, AXES, perm)  41 us
    ppermute x20, waiting for transfers between devices, move(): return lax.ppermute(array, AXES, perm)  9.96 us
    pallas_call x2, Pallas kernels, conv(): pl.pallas_call(functools.partial(conv_kernel, backward), out_shape=jax.Sh...  6.64 us
    pallas_call x1, Pallas kernels, side(): pl.pallas_call(side_kernel, out_shape=(PIECES, PIECES), in_specs=[SMEM, A...  3.28 us
    pallas_call x1, Pallas kernels, centre(): pl.pallas_call(centre_kernel, out_shape=(PIECES, PIECES), in_specs=[SMEM,...  2.1 us
  transfers between devices with their start and end apart: 20, of which 6 were waited for; matrix products, arithmetic and copies ran while one was open for 1% of the time, Pallas kernels for 15%

profile of v1, /device:TPU:1, one launch (start us, length us, event | category | flops | bytes accessed | tf_op | source)
XLA Modules:
  0.0 66.1 jit_solution(255282207141877385)
XLA Ops:
  0.6 0.1 pad_add_fusion.place
  0.7 0.9 %copy-done.1 = bf16[1,1,32,32,128]{4,3,2,1,0:T(8,128)(2,1)S(1)} copy-done((bf16[1,1,32,32,128]{4,3,2,1,0:T(8,128)(2,1)S(1)}, bf16[1,1,32,32,128]{4,3,2,1,0:T(8,128)(2,1)}, u32[]{:S(2)}) %copy-start.1) | copy-done | bytes 262168
  1.7 2.1 %centre.1 = (f32[4,3,16,384]{3,2,1,0:T(8,128)S(1)}, f32[4,3,16,384]{3,2,1,0:T(8,128)S(1)}) custom-call(s32[3]{0:T(128)S(1)} %pad_add_fusion.place, bf16[1024,128]{1,0:T(8,128)(2,1)} %bitcast.own.vol, bf16[1024,128]{1,0:T(8,128)(2,1)S(1)} %bitcast.34), custom_call_target="tpu_custom_call" | custom-call | flops 603979776 | bytes 4194304 | tf_op jit(solution)/shard_map/centre/pallas_call | solution.py:186
  3.8 3.3 %collective-permute-start.4 = (f32[4,3,16,384]{3,2,1,0:T(8,128)S(1)}, f32[4,3,16,384]{3,2,1,0:T(8,128)S(1)}, u32[]{:S(2)}, u32[]{:S(2)}) collective-permute-start(f32[4,3,16,384]{3,2,1,0:T(8,128)S(1)} %get-tuple-element.8), channel_id=1, source_target_pairs={{0,32},{1,33},{2,34},{3,35},{4,36},{5,37},{6,38},{7,39},{8,40},{9,... | collective-permute-start | bytes 884744 | tf_op jit(solution)/shard_map/ppermute | solution.py:32
  7.1 0.7 %collective-permute-start.2 = (bf16[1024,128]{1,0:T(8,128)(2,1)S(1)}, bf16[1024,128]{1,0:T(8,128)(2,1)S(1)}, u32[]{:S(2)}, u32[]{:S(2)}) collective-permute-start(bf16[1024,128]{1,0:T(8,128)(2,1)S(1)} %bitcast.35), channel_id=1, source_target_pairs={{1,2},{2,1},{3,4},{4,3},{5,6},{6,5},{7,8},{8,7},{9,10},{10,9},{11,... | collective-permute-start | bytes 786440 | tf_op jit(solution)/shard_map/ppermute | solution.py:32
  7.8 0.5 collective-permute-done.4
  8.4 8.1 %collective-permute-start.7 = (f32[3,16,384]{2,1,0:T(8,128)S(1)}, f32[3,16,384]{2,1,0:T(8,128)S(1)}, u32[]{:S(2)}, u32[]{:S(2)}) collective-permute-start(f32[3,16,384]{2,1,0:T(8,128)S(1)} %get-tuple-element.18), channel_id=1, source_target_pairs={{0,24},{1,25},{2,26},{3,27},{4,28},{5,29},{6,30},{7,31},{8,16},{9,... | collective-permute-start | bytes 221192 | tf_op jit(solution)/shard_map/ppermute | solution.py:32
  16.5 0.2 collective-permute-start.6
  16.7 0.5 collective-permute-start.5
  17.2 3.3 %side.1 = (f32[4,3,16,384]{3,2,1,0:T(8,128)S(1)}, f32[4,3,16,384]{3,2,1,0:T(8,128)S(1)}) custom-call(s32[3]{0:T(128)S(1)} %pad_add_fusion.place, bf16[1024,128]{1,0:T(8,128)(2,1)} %bitcast.own.vol, bf16[1024,128]{1,0:T(8,128)(2,1)S(1)} %bitcast.36, bf16[1024,128]{1,0:T(8,128)(2,1)S(1)} %collective-permute-done.1.near_vol, ...), custom_call_target="tpu_custom_call" | custom-call | flops 1207959552 | bytes 8388608 | tf_op jit(solution)/shard_map/side/pallas_call | solution.py:204
  20.5 1.3 %collective-permute-start.8 = (f32[4,3,16,384]{3,2,1,0:T(8,128)S(1)}, f32[4,3,16,384]{3,2,1,0:T(8,128)S(1)}, u32[]{:S(2)}, u32[]{:S(2)}) collective-permute-start(f32[4,3,16,384]{3,2,1,0:T(8,128)S(1)} %get-tuple-element.10), channel_id=1, source_target_pairs={{0,32},{1,33},{2,34},{3,35},{4,36},{5,37},{6,38},{7,39},{8,40},{9,... | collective-permute-start | bytes 884744 | tf_op jit(solution)/shard_map/ppermute | solution.py:32
  21.8 0.7 %collective-permute-start = (bf16[1024,128]{1,0:T(8,128)(2,1)}, bf16[1024,128]{1,0:T(8,128)(2,1)S(1)}, u32[]{:S(2)}, u32[]{:S(2)}) collective-permute-start(bf16[1024,128]{1,0:T(8,128)(2,1)} %bitcast.own.vol), channel_id=1, source_target_pairs={{1,2},{2,1},{3,4},{4,3},{5,6},{6,5},{7,8},{8,7},{9,10},{10,9},{11,... | collective-permute-start | bytes 786440 | tf_op jit(solution)/shard_map/ppermute | solution.py:32
  22.5 3.8 %collective-permute-start.3 = (bf16[1024,128]{1,0:T(8,128)(2,1)S(1)}, bf16[1024,128]{1,0:T(8,128)(2,1)S(1)}, u32[]{:S(2)}, u32[]{:S(2)}) collective-permute-start(bf16[1024,128]{1,0:T(8,128)(2,1)S(1)} %bitcast.37), channel_id=1, source_target_pairs={{0,1},{1,0},{2,3},{3,2},{4,5},{5,4},{6,7},{7,6},{8,9},{9,8},{10,11... | collective-permute-start | bytes 786440 | tf_op jit(solution)/shard_map/ppermute | solution.py:32
  26.4 6.5 %collective-permute-start.11 = (f32[3,16,384]{2,1,0:T(8,128)S(1)}, f32[3,16,384]{2,1,0:T(8,128)S(1)}, u32[]{:S(2)}, u32[]{:S(2)}) collective-permute-start(f32[3,16,384]{2,1,0:T(8,128)S(1)} %get-tuple-element.15), channel_id=1, source_target_pairs={{0,24},{1,25},{2,26},{3,27},{4,28},{5,29},{6,30},{7,31},{8,16},{9,... | collective-permute-start | bytes 221192 | tf_op jit(solution)/shard_map/ppermute | solution.py:32
  32.9 0.2 collective-permute-start.10
  33.1 0.4 collective-permute-start.9
  33.6 2.1 %collective-permute-done.11 = f32[3,16,384]{2,1,0:T(8,128)S(1)} collective-permute-done((f32[3,16,384]{2,1,0:T(8,128)S(1)}, f32[3,16,384]{2,1,0:T(8,128)S(1)}, u32[]{:S(2)}, u32[]{:S(2)}) %collective-permute-start.11) | collective-permute-done | bytes 73760 | tf_op jit(solution)/shard_map/ppermute | solution.py:32
  35.7 5.1 %collective-permute-done.10 = f32[3,16,384]{2,1,0:T(8,128)S(1)} collective-permute-done((f32[3,16,384]{2,1,0:T(8,128)S(1)}, f32[3,16,384]{2,1,0:T(8,128)S(1)}, u32[]{:S(2)}, u32[]{:S(2)}) %collective-permute-start.10) | collective-permute-done | bytes 73760 | tf_op jit(solution)/shard_map/ppermute | solution.py:32
  41.0 0.1 collective-permute-start.13
  41.1 0.7 %collective-permute-start.14 = (f32[24,384]{1,0:T(8,128)S(1)}, f32[24,384]{1,0:T(8,128)S(1)}, u32[]{:S(2)}, u32[]{:S(2)}) collective-permute-start(f32[24,384]{1,0:T(8,128)S(1)} %reshape_squeeze.15), channel_id=1, source_target_pairs={{0,6},{1,7},{2,4},{3,5},{4,2},{5,3},{6,0},{7,1},{8,14},{9,15},{10,... | collective-permute-start | bytes 110600 | tf_op jit(solution)/shard_map/ppermute | solution.py:32
  41.8 4.9 %collective-permute-start.12 = (f32[24,384]{1,0:T(8,128)S(1)}, f32[24,384]{1,0:T(8,128)S(1)}, u32[]{:S(2)}, u32[]{:S(2)}) collective-permute-start(f32[24,384]{1,0:T(8,128)S(1)} %reshape_squeeze.13), channel_id=1, source_target_pairs={{0,2},{1,3},{2,0},{3,1},{4,6},{5,7},{6,4},{7,5},{8,10},{9,11},{10,... | collective-permute-start | bytes 110600 | tf_op jit(solution)/shard_map/ppermute | solution.py:32
  46.8 1.0 %collective-permute-done.13 = f32[24,384]{1,0:T(8,128)S(1)} collective-permute-done((f32[24,384]{1,0:T(8,128)S(1)}, f32[24,384]{1,0:T(8,128)S(1)}, u32[]{:S(2)}, u32[]{:S(2)}) %collective-permute-start.13) | collective-permute-done | bytes 36896 | tf_op jit(solution)/shard_map/ppermute | solution.py:32
  47.8 0.6 collective-permute-done.12
  48.4 2.8 %collective-permute-start.17 = (f32[24,384]{1,0:T(8,128)S(1)}, f32[24,384]{1,0:T(8,128)S(1)}, u32[]{:S(2)}, u32[]{:S(2)}) collective-permute-start(f32[24,384]{1,0:T(8,128)S(1)} %add_add_fusion.1), channel_id=1, source_target_pairs={{0,192},{1,193},{2,194},{3,195},{4,196},{5,197},{6,198},{7,199},{8... | collective-permute-start | bytes 110600 | tf_op jit(solution)/shard_map/ppermute | solution.py:32
  51.2 0.3 collective-permute-start.16
  51.6 0.3 collective-permute-start.15
  51.9 3.0 %grad_volume.1 = bf16[1024,128]{1,0:T(8,128)(2,1)} custom-call(bf16[27,128,128]{2,1,0:T(8,128)(2,1)S(1)} %copy-done, bf16[1024,128]{1,0:T(8,128)(2,1)S(1)} %get-tuple-element.12.before, bf16[1024,128]{1,0:T(8,128)(2,1)S(1)} %bitcast.38, bf16[1024,128]{1,0:T(8,128)(2,1)S(1)} %get-tuple-element.11.after), custom_call_target="tpu_custom_call" | custom-call | flops 1811939328 | bytes 8388608 | tf_op jit(solution)/shard_map/grad_volume/pallas_call | solution.py:222
  54.9 0.7 collective-permute-done.16
  55.6 6.0 %collective-permute-start.19 = (f32[24,384]{1,0:T(8,128)S(1)}, f32[24,384]{1,0:T(8,128)S(1)}, u32[]{:S(2)}, u32[]{:S(2)}) collective-permute-start(f32[24,384]{1,0:T(8,128)S(1)} %add_add_fusion), channel_id=1, source_target_pairs={{1,32},{3,34},{5,36},{7,38},{9,40},{11,42},{13,44},{15,46},{17,48}... | collective-permute-start | bytes 110600 | tf_op jit(solution)/shard_map/ppermute | solution.py:32
  61.6 0.1 collective-permute-start.18
  61.7 3.7 %response.1 = bf16[1024,128]{1,0:T(8,128)(2,1)} custom-call(bf16[27,128,128]{2,1,0:T(8,128)(2,1)S(1)} %copy-done, bf16[1024,128]{1,0:T(8,128)(2,1)S(1)} %get-tuple-element.30.before, bf16[1024,128]{1,0:T(8,128)(2,1)} %bitcast.own.vol, bf16[1024,128]{1,0:T(8,128)(2,1)S(1)} %get-tuple-element.31.after), custom_call_target="tpu_custom_call" | custom-call | flops 1811939328 | bytes 8388608 | tf_op jit(solution)/shard_map/response/pallas_call | solution.py:222
  65.5 0.6 copy.6
  (44 shorter events, 0.5 us)
Async XLA Ops:
  0.7 1.0 %copy-start.1 = (bf16[1,1,32,32,128]{4,3,2,1,0:T(8,128)(2,1)S(1)}, bf16[1,1,32,32,128]{4,3,2,1,0:T(8,128)(2,1)}, u32[]{:S(2)}) copy-start(bf16[1,1,32,32,128]{4,3,2,1,0:T(8,128)(2,1)} %param.5) | copy-start | bytes 786436
  3.8 4.5 %collective-permute-start.4 = (f32[4,3,16,384]{3,2,1,0:T(8,128)S(1)}, f32[4,3,16,384]{3,2,1,0:T(8,128)S(1)}, u32[]{:S(2)}, u32[]{:S(2)}) collective-permute-start(f32[4,3,16,384]{3,2,1,0:T(8,128)S(1)} %get-tuple-element.8), channel_id=1, source_target_pairs={{0,32},{1,33},{2,34},{3,35},{4,36},{5,37},{6,38},{7,39},{8,40},{9,... | collective-permute-start | bytes 884744 | tf_op jit(solution)/shard_map/ppermute | solution.py:32
  7.1 10.1 %collective-permute-start.1 = (bf16[1024,128]{1,0:T(8,128)(2,1)}, bf16[1024,128]{1,0:T(8,128)(2,1)S(1)}, u32[]{:S(2)}, u32[]{:S(2)}) collective-permute-start(bf16[1024,128]{1,0:T(8,128)(2,1)} %bitcast.own.vol), channel_id=1, source_target_pairs={{0,1},{1,0},{2,3},{3,2},{4,5},{5,4},{6,7},{7,6},{8,9},{9,8},{10,11... | collective-permute-start | bytes 786440 | tf_op jit(solution)/shard_map/ppermute | solution.py:32
  7.1 10.1 %collective-permute-start.2 = (bf16[1024,128]{1,0:T(8,128)(2,1)S(1)}, bf16[1024,128]{1,0:T(8,128)(2,1)S(1)}, u32[]{:S(2)}, u32[]{:S(2)}) collective-permute-start(bf16[1024,128]{1,0:T(8,128)(2,1)S(1)} %bitcast.35), channel_id=1, source_target_pairs={{1,2},{2,1},{3,4},{4,3},{5,6},{6,5},{7,8},{8,7},{9,10},{10,9},{11,... | collective-permute-start | bytes 786440 | tf_op jit(solution)/shard_map/ppermute | solution.py:32
  8.4 14.1 %collective-permute-start.7 = (f32[3,16,384]{2,1,0:T(8,128)S(1)}, f32[3,16,384]{2,1,0:T(8,128)S(1)}, u32[]{:S(2)}, u32[]{:S(2)}) collective-permute-start(f32[3,16,384]{2,1,0:T(8,128)S(1)} %get-tuple-element.18), channel_id=1, source_target_pairs={{0,24},{1,25},{2,26},{3,27},{4,28},{5,29},{6,30},{7,31},{8,16},{9,... | collective-permute-start | bytes 221192 | tf_op jit(solution)/shard_map/ppermute | solution.py:32
  16.5 9.8 %collective-permute-start.6 = (f32[3,16,384]{2,1,0:T(8,128)S(1)}, f32[3,16,384]{2,1,0:T(8,128)S(1)}, u32[]{:S(2)}, u32[]{:S(2)}) collective-permute-start(f32[3,16,384]{2,1,0:T(8,128)S(1)} %get-tuple-element.19), channel_id=1, source_target_pairs={{0,16},{1,17},{2,18},{3,19},{4,20},{5,21},{6,22},{7,23},{8,24},{9,... | collective-permute-start | bytes 221192 | tf_op jit(solution)/shard_map/ppermute | solution.py:32
  16.7 5.7 %copy-start.2 = (bf16[1,1,32,32,128]{4,3,2,1,0:T(8,128)(2,1)S(1)}, bf16[1,1,32,32,128]{4,3,2,1,0:T(8,128)(2,1)}, u32[]{:S(2)}) copy-start(bf16[1,1,32,32,128]{4,3,2,1,0:T(8,128)(2,1)} %param.5) | copy-start | bytes 786436
  16.7 9.6 %collective-permute-start.5 = (f32[3,16,384]{2,1,0:T(8,128)S(1)}, f32[3,16,384]{2,1,0:T(8,128)S(1)}, u32[]{:S(2)}, u32[]{:S(2)}) collective-permute-start(f32[3,16,384]{2,1,0:T(8,128)S(1)} %get-tuple-element.20), channel_id=1, source_target_pairs={{0,8},{1,9},{2,10},{3,11},{4,12},{5,13},{6,14},{7,15},{8,0},{9,1},... | collective-permute-start | bytes 221192 | tf_op jit(solution)/shard_map/ppermute | solution.py:32
  20.5 5.9 %collective-permute-start.8 = (f32[4,3,16,384]{3,2,1,0:T(8,128)S(1)}, f32[4,3,16,384]{3,2,1,0:T(8,128)S(1)}, u32[]{:S(2)}, u32[]{:S(2)}) collective-permute-start(f32[4,3,16,384]{3,2,1,0:T(8,128)S(1)} %get-tuple-element.10), channel_id=1, source_target_pairs={{0,32},{1,33},{2,34},{3,35},{4,36},{5,37},{6,38},{7,39},{8,40},{9,... | collective-permute-start | bytes 884744 | tf_op jit(solution)/shard_map/ppermute | solution.py:32
  21.8 25.0 %collective-permute-start = (bf16[1024,128]{1,0:T(8,128)(2,1)}, bf16[1024,128]{1,0:T(8,128)(2,1)S(1)}, u32[]{:S(2)}, u32[]{:S(2)}) collective-permute-start(bf16[1024,128]{1,0:T(8,128)(2,1)} %bitcast.own.vol), channel_id=1, source_target_pairs={{1,2},{2,1},{3,4},{4,3},{5,6},{6,5},{7,8},{8,7},{9,10},{10,9},{11,... | collective-permute-start | bytes 786440 | tf_op jit(solution)/shard_map/ppermute | solution.py:32
  22.5 24.3 %collective-permute-start.3 = (bf16[1024,128]{1,0:T(8,128)(2,1)S(1)}, bf16[1024,128]{1,0:T(8,128)(2,1)S(1)}, u32[]{:S(2)}, u32[]{:S(2)}) collective-permute-start(bf16[1024,128]{1,0:T(8,128)(2,1)S(1)} %bitcast.37), channel_id=1, source_target_pairs={{0,1},{1,0},{2,3},{3,2},{4,5},{5,4},{6,7},{7,6},{8,9},{9,8},{10,11... | collective-permute-start | bytes 786440 | tf_op jit(solution)/shard_map/ppermute | solution.py:32
  26.4 9.2 %collective-permute-start.11 = (f32[3,16,384]{2,1,0:T(8,128)S(1)}, f32[3,16,384]{2,1,0:T(8,128)S(1)}, u32[]{:S(2)}, u32[]{:S(2)}) collective-permute-start(f32[3,16,384]{2,1,0:T(8,128)S(1)} %get-tuple-element.15), channel_id=1, source_target_pairs={{0,24},{1,25},{2,26},{3,27},{4,28},{5,29},{6,30},{7,31},{8,16},{9,... | collective-permute-start | bytes 221192 | tf_op jit(solution)/shard_map/ppermute | solution.py:32
  32.9 7.9 %collective-permute-start.10 = (f32[3,16,384]{2,1,0:T(8,128)S(1)}, f32[3,16,384]{2,1,0:T(8,128)S(1)}, u32[]{:S(2)}, u32[]{:S(2)}) collective-permute-start(f32[3,16,384]{2,1,0:T(8,128)S(1)} %get-tuple-element.16), channel_id=1, source_target_pairs={{0,16},{1,17},{2,18},{3,19},{4,20},{5,21},{6,22},{7,23},{8,24},{9,... | collective-permute-start | bytes 221192 | tf_op jit(solution)/shard_map/ppermute | solution.py:32
  33.1 7.7 %collective-permute-start.9 = (f32[3,16,384]{2,1,0:T(8,128)S(1)}, f32[3,16,384]{2,1,0:T(8,128)S(1)}, u32[]{:S(2)}, u32[]{:S(2)}) collective-permute-start(f32[3,16,384]{2,1,0:T(8,128)S(1)} %get-tuple-element.17), channel_id=1, source_target_pairs={{0,8},{1,9},{2,10},{3,11},{4,12},{5,13},{6,14},{7,15},{8,0},{9,1},... | collective-permute-start | bytes 221192 | tf_op jit(solution)/shard_map/ppermute | solution.py:32
  41.0 10.9 %copy-start = (bf16[27,128,128]{2,1,0:T(8,128)(2,1)S(1)}, bf16[27,128,128]{2,1,0:T(8,128)(2,1)}, u32[]{:S(2)}) copy-start(bf16[27,128,128]{2,1,0:T(8,128)(2,1)} %weights.3) | copy-start | bytes 2654212
  41.0 6.8 %collective-permute-start.13 = (f32[24,384]{1,0:T(8,128)S(1)}, f32[24,384]{1,0:T(8,128)S(1)}, u32[]{:S(2)}, u32[]{:S(2)}) collective-permute-start(f32[24,384]{1,0:T(8,128)S(1)} %reshape_squeeze.14), channel_id=1, source_target_pairs={{0,4},{1,5},{2,6},{3,7},{4,0},{5,1},{6,2},{7,3},{8,12},{9,13},{10,... | collective-permute-start | bytes 110600 | tf_op jit(solution)/shard_map/ppermute | solution.py:32
  41.1 6.7 %collective-permute-start.14 = (f32[24,384]{1,0:T(8,128)S(1)}, f32[24,384]{1,0:T(8,128)S(1)}, u32[]{:S(2)}, u32[]{:S(2)}) collective-permute-start(f32[24,384]{1,0:T(8,128)S(1)} %reshape_squeeze.15), channel_id=1, source_target_pairs={{0,6},{1,7},{2,4},{3,5},{4,2},{5,3},{6,0},{7,1},{8,14},{9,15},{10,... | collective-permute-start | bytes 110600 | tf_op jit(solution)/shard_map/ppermute | solution.py:32
  41.8 6.6 %collective-permute-start.12 = (f32[24,384]{1,0:T(8,128)S(1)}, f32[24,384]{1,0:T(8,128)S(1)}, u32[]{:S(2)}, u32[]{:S(2)}) collective-permute-start(f32[24,384]{1,0:T(8,128)S(1)} %reshape_squeeze.13), channel_id=1, source_target_pairs={{0,2},{1,3},{2,0},{3,1},{4,6},{5,7},{6,4},{7,5},{8,10},{9,11},{10,... | collective-permute-start | bytes 110600 | tf_op jit(solution)/shard_map/ppermute | solution.py:32
  48.4 6.5 %collective-permute-start.17 = (f32[24,384]{1,0:T(8,128)S(1)}, f32[24,384]{1,0:T(8,128)S(1)}, u32[]{:S(2)}, u32[]{:S(2)}) collective-permute-start(f32[24,384]{1,0:T(8,128)S(1)} %add_add_fusion.1), channel_id=1, source_target_pairs={{0,192},{1,193},{2,194},{3,195},{4,196},{5,197},{6,198},{7,199},{8... | collective-permute-start | bytes 110600 | tf_op jit(solution)/shard_map/ppermute | solution.py:32
  51.2 4.3 %collective-permute-start.16 = (f32[24,384]{1,0:T(8,128)S(1)}, f32[24,384]{1,0:T(8,128)S(1)}, u32[]{:S(2)}, u32[]{:S(2)}) collective-permute-start(f32[24,384]{1,0:T(8,128)S(1)} %add_add_fusion.1), channel_id=1, source_target_pairs={{0,128},{1,129},{2,130},{3,131},{4,132},{5,133},{6,134},{7,135},{8... | collective-permute-start | bytes 110600 | tf_op jit(solution)/shard_map/ppermute | solution.py:32
  51.6 4.0 %collective-permute-start.15 = (f32[24,384]{1,0:T(8,128)S(1)}, f32[24,384]{1,0:T(8,128)S(1)}, u32[]{:S(2)}, u32[]{:S(2)}) collective-permute-start(f32[24,384]{1,0:T(8,128)S(1)} %add_add_fusion.1), channel_id=1, source_target_pairs={{0,64},{1,65},{2,66},{3,67},{4,68},{5,69},{6,70},{7,71},{8,72},{9,... | collective-permute-start | bytes 110600 | tf_op jit(solution)/shard_map/ppermute | solution.py:32
  55.6 9.8 %collective-permute-start.19 = (f32[24,384]{1,0:T(8,128)S(1)}, f32[24,384]{1,0:T(8,128)S(1)}, u32[]{:S(2)}, u32[]{:S(2)}) collective-permute-start(f32[24,384]{1,0:T(8,128)S(1)} %add_add_fusion), channel_id=1, source_target_pairs={{1,32},{3,34},{5,36},{7,38},{9,40},{11,42},{13,44},{15,46},{17,48}... | collective-permute-start | bytes 110600 | tf_op jit(solution)/shard_map/ppermute | solution.py:32
  61.6 3.8 %collective-permute-start.18 = (f32[24,384]{1,0:T(8,128)S(1)}, f32[24,384]{1,0:T(8,128)S(1)}, u32[]{:S(2)}, u32[]{:S(2)}) collective-permute-start(f32[24,384]{1,0:T(8,128)S(1)} %add_add_fusion), channel_id=1, source_target_pairs={{0,32},{1,0},{2,34},{3,2},{4,36},{5,4},{6,38},{7,6},{8,40},{9,8},{... | collective-permute-start | bytes 110600 | tf_op jit(solution)/shard_map/ppermute | solution.py:32

commit v2 on v1

v2 whole, which is shorter than its diff:
```python
import functools
import math

import jax
import jax.numpy as jnp
from jax import lax
from jax.experimental import pallas as pl
from jax.experimental.pallas import tpu as pltpu
from jax.sharding import PartitionSpec as P

AXES = ("sample", "slab")
YS, CORES, XS, ZS = 4, 2, 4, 8
GRID, CELLS, C = 32, 1024, 128
PADDED = CELLS + 2 * GRID
F32, BF16 = jnp.float32, jnp.bfloat16
ANY = pl.BlockSpec(memory_space=pl.ANY)
HBM = pl.BlockSpec(memory_space=pltpu.HBM)
VMEM = pl.BlockSpec(memory_space=pltpu.VMEM)
SMEM = pl.BlockSpec(memory_space=pltpu.SMEM)


def move(array, target):
    perm = []
    for y in range(YS):
        for core in range(CORES):
            for slab in range(XS * ZS):
                to = target(y, core, slab)
                if to is not None:
                    ty, tcore, tslab = to
                    perm.append(
                        ((y * CORES + core) * XS * ZS + slab, (ty * CORES + tcore) * XS * ZS + tslab)
                    )
    return lax.ppermute(array, AXES, perm)


def partner(y, core, slab):
    return y, core, slab ^ 1


def other(y, core, slab):
    to = slab - 1 if slab % 2 == 0 else slab + 1
    return (y, core, to) if 0 <= to < XS * ZS else None


def across_x(s):
    return lambda y, core, slab: (y, core, slab ^ (s * ZS))


def across_y(s):
    return lambda y, core, slab: (y ^ s, core, slab)


def zero_edges(padded):
    padded[0:GRID] = jnp.zeros((GRID, C), BF16)
    padded[GRID + CELLS : PADDED] = jnp.zeros((GRID, C), BF16)


def row_order(place):
    r = lax.broadcasted_iota(jnp.int32, (C, C), 0)
    o = lax.broadcasted_iota(jnp.int32, (C, C), 1)
    half, s, t, j = r >> 6, (r >> 4) & 3, (r >> 2) & 3, r & 3
    wanted = ((place[1] ^ s) << 5) + ((place[2] ^ t) << 3) + ((place[0] ^ half) << 2) + j
    return jnp.where(o == wanted, 1.0, 0.0).astype(BF16)


def fill_rows(rows, order, cot):
    k = lax.broadcasted_iota(jnp.int32, (256, 256), 0)
    n = lax.broadcasted_iota(jnp.int32, (256, 256), 1)
    same = (k >> 5) == (n >> 5)
    left = jnp.where(same & (k == n + 1), 1.0, 0.0).astype(BF16)
    right = jnp.where(same & (k == n - 1), 1.0, 0.0).astype(BF16)
    for block in range(0, CELLS, 256):
        cells = slice(block, block + 256)
        turned = lax.dot_general(
            order, cot[cells], (((1,), (1,)), ((), ())), preferred_element_type=F32
        ).astype(BF16)
        rows[0:C, cells] = jnp.dot(turned, left, preferred_element_type=F32).astype(BF16)
        rows[C : 2 * C, cells] = turned
        rows[2 * C : 3 * C, cells] = jnp.dot(turned, right, preferred_element_type=F32).astype(BF16)


def product(rows, padded):
    wide = jnp.concatenate([padded[b * GRID : b * GRID + CELLS] for b in range(3)], axis=1)
    return jnp.dot(rows[...], wide, preferred_element_type=F32)


def write_pieces(total, keep, send, slot):
    for s in range(4):
        for c in range(3):
            start = c * C + s * 16
            keep[s, slot + c] = total[start : start + 16]
            send[s, slot + c] = total[start + 64 : start + 80]


def centre_kernel(place, vol, cot, keep, send, rows, padded, cots, sems):
    copies = [
        pltpu.make_async_copy(cot, cots, sems.at[0]),
        pltpu.make_async_copy(vol, padded.at[pl.ds(GRID, CELLS)], sems.at[1]),
    ]
    for copy in copies:
        copy.start()
    zero_edges(padded)
    order = row_order(place)
    copies[0].wait()
    fill_rows(rows, order, cots)
    copies[1].wait()
    write_pieces(product(rows, padded), keep, send, 0)


def side_kernel(
    place, vol, near_vol, near_cot, own_rows, keep0, send0, keep, send, padded, cots, rows, sems
):
    copies = [
        pltpu.make_async_copy(near_cot, cots, sems.at[0]),
        pltpu.make_async_copy(near_vol, padded.at[0, pl.ds(GRID, CELLS)], sems.at[1]),
        pltpu.make_async_copy(vol, padded.at[1, pl.ds(GRID, CELLS)], sems.at[2]),
    ]
    for copy in copies:
        copy.start()
    keep[:, 0:3] = keep0[...]
    send[:, 0:3] = send0[...]
    zero_edges(padded.at[0])
    zero_edges(padded.at[1])
    order = row_order(place)
    copies[0].wait()
    fill_rows(rows, order, cots)
    copies[1].wait()
    copies[2].wait()
    total = product(own_rows, padded.at[0]) + product(rows, padded.at[1])
    write_pieces(total, keep, send, 3)


def conv_kernel(backward, place, weights, partner_plane, own, other_plane, out, padded, weight, sems):
    after = 2 - 2 * place[3]
    partner_at = 2 - after if backward else after
    copies = [
        pltpu.make_async_copy(partner_plane, padded.at[partner_at, pl.ds(GRID, CELLS)], sems.at[0]),
        pltpu.make_async_copy(own, padded.at[1, pl.ds(GRID, CELLS)], sems.at[1]),
        pltpu.make_async_copy(other_plane, padded.at[2 - partner_at, pl.ds(GRID, CELLS)], sems.at[2]),
        pltpu.make_async_copy(weights, weight, sems.at[3]),
    ]
    for copy in copies:
        copy.start()
    for a in range(3):
        zero_edges(padded.at[a])
    for copy in copies:
        copy.wait()
    pairs = [tuple(range(9))]

    @pl.loop(0, CELLS // 1024)
    def _(block):
        start = pl.multiple_of(block * 1024, 1024)
        total = None
        for pair in pairs:
            left, right = [], []
            for ab in pair:
                a, b = ab // 3, ab % 3
                shift = (2 - b if backward else b) * GRID
                left.append(padded[a, pl.ds(pl.multiple_of(start + shift, GRID), 1024), :])
                right.append(
                    jnp.concatenate([weight[3 * ab + c] for c in range(3)], axis=0 if backward else 1)
                )
            lhs = jnp.concatenate(left, axis=1)
            rhs = jnp.concatenate(right, axis=1 if backward else 0)
            dims = (((1,), (1 if backward else 0,)), ((), ()))
            part = lax.dot_general(lhs, rhs, dims, preferred_element_type=F32)
            total = part if total is None else total + part
        low, mid, high = total[:, :C], total[:, C : 2 * C], total[:, 2 * C :]
        if backward:
            low, high = high, low
        x = lax.broadcasted_iota(jnp.int32, (1024, C), 0) & (GRID - 1)
        low = jnp.where(x == 0, 0.0, pltpu.roll(low, 1, 0))
        high = jnp.where(x == GRID - 1, 0.0, pltpu.roll(high, 1024 - 1, 0))
        out[pl.ds(start, 1024), :] = (mid + low + high).astype(BF16)


HALF = jax.ShapeDtypeStruct((4, 3, 16, 3 * C), F32)
WHOLE = jax.ShapeDtypeStruct((4, 6, 16, 3 * C), F32)
ROWS = jax.ShapeDtypeStruct((3 * C, CELLS), BF16)
COST = pl.CostEstimate(flops=1 << 20, bytes_accessed=1 << 16, transcendentals=0)
PARAMS = pltpu.CompilerParams(vmem_limit_bytes=32 * 1024 * 1024)


def centre(place, vol, cot):
    return pl.pallas_call(
        centre_kernel,
        out_shape=(HALF, HALF, ROWS),
        in_specs=[SMEM, HBM, HBM],
        out_specs=(VMEM, VMEM, VMEM),
        scratch_shapes=[
            pltpu.VMEM((PADDED, C), BF16),
            pltpu.VMEM((CELLS, C), BF16),
            pltpu.SemaphoreType.DMA((2,)),
        ],
        compiler_params=PARAMS,
        cost_estimate=COST,
        name="centre",
    )(place, vol, cot)


def side(place, vol, near_vol, near_cot, rows, keep, send):
    return pl.pallas_call(
        side_kernel,
        out_shape=(WHOLE, WHOLE),
        in_specs=[SMEM, HBM, ANY, ANY, VMEM, VMEM, VMEM],
        out_specs=(VMEM, VMEM),
        scratch_shapes=[
            pltpu.VMEM((2, PADDED, C), BF16),
            pltpu.VMEM((CELLS, C), BF16),
            pltpu.VMEM((3 * C, CELLS), BF16),
            pltpu.SemaphoreType.DMA((3,)),
        ],
        compiler_params=PARAMS,
        cost_estimate=COST,
        name="side",
    )(place, vol, near_vol, near_cot, rows, keep, send)


def conv(backward, place, weights, partner_plane, own, other_plane):
    return pl.pallas_call(
        functools.partial(conv_kernel, backward),
        out_shape=jax.ShapeDtypeStruct((CELLS, C), BF16),
        in_specs=[SMEM, ANY, ANY, HBM, ANY],
        out_specs=VMEM,
        scratch_shapes=[
            pltpu.VMEM((3, PADDED, C), BF16),
            pltpu.VMEM((27, C, C), BF16),
            pltpu.SemaphoreType.DMA((4,)),
        ],
        compiler_params=PARAMS,
        cost_estimate=COST,
        name="grad_volume" if backward else "response",
    )(place, weights, partner_plane, own, other_plane)


def after(value, *earlier):
    return lax.optimization_barrier((value, *earlier))[0]


def on_device(volume, kernel, cotangent):
    sample, slab = lax.axis_index("sample"), lax.axis_index("slab")
    core, z_odd = sample & 1, slab & 1
    place = jnp.stack([core, slab >> 3, (slab >> 1) & 3, z_odd]).astype(jnp.int32)
    scale = 1.0 / math.sqrt(YS * CORES * XS * ZS * CELLS)
    vol, cot = volume.reshape(CELLS, C), cotangent.reshape(CELLS, C)
    swap = lambda y, c, s: (y, 1 - c, s)

    other_cot = move(cot, other)
    other_vol = move(vol, other)
    partner_vol = move(vol, partner)
    partner_cot = move(cot, partner)
    keep, send, rows = centre(place, vol, cot)
    keep, send = side(place, vol, partner_vol, other_cot, rows, keep, send)
    total = keep + move(after(send, other_vol, partner_cot), swap)

    away = total[1:]
    peak = jnp.max(jnp.abs(away), axis=(1, 3), keepdims=True)
    power = jnp.clip(jnp.ceil(jnp.log2(peak)), -100.0, 100.0)
    scaled = (away * jnp.exp2(-power)).astype(jnp.float16)
    powers = jnp.broadcast_to(power, (3, 1, 16, 3 * C)).astype(jnp.float16)
    packed = jnp.concatenate([scaled, powers], axis=1)
    parts = [move(packed[s - 1], across_x(s)) for s in range(1, 4)]
    parts = [p[:6].astype(F32) * jnp.exp2(p[6:].astype(F32)) for p in parts]
    grad_volume = conv(True, after(place, total), kernel, partner_cot, cot, other_cot)
    total = total[0] + parts[0] + (parts[1] + parts[2])
    total = after(total, grad_volume)

    pieces = [total.reshape(6, 4, 4, 3 * C)[:, t].reshape(24, 3 * C) for t in range(4)]

    def to_owner(t):
        return lambda y, c, s: (y, s & 1, ((s ^ (2 * t)) & ~1) | c)

    parts = [move(pieces[t], to_owner(t)) for t in range(4)]
    response = conv(False, after(place, total), kernel, partner_vol, vol, other_vol)
    total = (parts[0] + parts[1]) + (parts[2] + parts[3])
    total = after(total, response)

    for s in (1, 3):
        total = total + move(total, across_y(s))
    twin = move(total, swap)
    from_even = jnp.where(core == 0, total, twin).reshape(2, 3, 4, 3, C)
    from_odd = jnp.where(core == 0, twin, total).reshape(2, 3, 4, 3, C)
    taps = jnp.stack([from_odd[1], from_even[0] + from_odd[0], from_even[1]])
    grad_kernel = (taps.transpose(2, 0, 3, 1, 4) * scale).reshape(4, 27, C)
    return (response.reshape(volume.shape), grad_volume.reshape(volume.shape), grad_kernel)


def solution(mesh):
    planes = P("sample", "slab", None, None, None)
    return jax.shard_map(
        on_device,
        mesh=mesh,
        in_specs=(planes, P(), planes),
        out_specs=(planes, planes, P("slab", None, None)),
        check_vma=False,
    )
```

time: 66.4 us -> 57.1 us (0.86)
  starting transfers between devices: 41 us -> 34 us
  waiting for transfers between devices: 9.96 us -> 8.2 us
  Pallas kernels: 12 us -> 10.5 us
  local copies, waits for them, and re-layouts: 1.83 us -> 2.79 us
    ppermute x20 -> x15, starting transfers between devices: 41 us -> 34 us  [move(): return lax.ppermute(array, AXES, perm)]
    ppermute x20 -> x15, waiting for transfers between devices: 9.96 us -> 8.2 us  [move(): return lax.ppermute(array, AXES, perm)]
    unnamed x7 -> x8, local copies, waits for them, and re-layouts: 0.97 us -> 1.91 us
    pallas_call x2, Pallas kernels: 5.38 us -> 4.51 us  [the longest x1 2.48 us: side(): pl.pallas_call(side_kernel, out_shape=(WHOLE, WHOLE), in_specs=[SMEM, HBM...]
    pallas_call x2, Pallas kernels: 6.64 us -> 5.97 us  [conv(): pl.pallas_call(functools.partial(conv_kernel, backward), out_shape=jax.Sh...]
  transfers between devices with their start and end apart: 20 -> 15, of which waited for: 6 -> 6; matrix products, arithmetic and copies ran while one was open for 1% -> 0% of each run, Pallas kernels for 15% -> 18%
where the time goes in v2:
time: 57.1 us; the launch traced here: 56.9 us
  starting transfers between devices  34 us (60%)
  Pallas kernels  10.5 us (18%)
  waiting for transfers between devices  8.2 us (14%)
  local copies, waits for them, and re-layouts  2.79 us (5%)
  between operations  0.89 us (2%)
  other arithmetic  0.61 us (1%)
    ppermute x15, starting transfers between devices, move(): return lax.ppermute(array, AXES, perm)  34 us
    ppermute x15, waiting for transfers between devices, move(): return lax.ppermute(array, AXES, perm)  8.2 us
    pallas_call x2, Pallas kernels, conv(): pl.pallas_call(functools.partial(conv_kernel, backward), out_shape=jax.Sh...  5.97 us
    pallas_call x1, Pallas kernels, side(): pl.pallas_call(side_kernel, out_shape=(WHOLE, WHOLE), in_specs=[SMEM, HBM...  2.48 us
    pallas_call x1, Pallas kernels, centre(): pl.pallas_call(centre_kernel, out_shape=(HALF, HALF, ROWS), in_specs=[SME...  2.02 us
    unnamed x8, local copies, waits for them, and re-layouts  1.91 us
  transfers between devices with their start and end apart: 15, of which 6 were waited for; matrix products, arithmetic and copies ran while one was open for 0% of the time, Pallas kernels for 18%

profile of v2, /device:TPU:1, one launch (start us, length us, event | category | flops | bytes accessed | tf_op | source)
XLA Modules:
  0.0 56.9 jit_solution(1769278956410438717)
XLA Ops:
  0.6 2.6 %collective-permute-start = (bf16[1024,128]{1,0:T(8,128)(2,1)}, bf16[1024,128]{1,0:T(8,128)(2,1)S(1)}, u32[]{:S(2)}, u32[]{:S(2)}) collective-permute-start(bf16[1024,128]{1,0:T(8,128)(2,1)} %bitcast.29), channel_id=1, source_target_pairs={{0,1},{1,0},{2,3},{3,2},{4,5},{5,4},{6,7},{7,6},{8,9},{9,8},{10,11... | collective-permute-start | bytes 786440 | tf_op jit(solution)/shard_map/ppermute | solution.py:33
  3.2 0.7 %collective-permute-start.1 = (bf16[1024,128]{1,0:T(8,128)(2,1)}, bf16[1024,128]{1,0:T(8,128)(2,1)S(1)}, u32[]{:S(2)}, u32[]{:S(2)}) collective-permute-start(bf16[1024,128]{1,0:T(8,128)(2,1)} %bitcast.34), channel_id=1, source_target_pairs={{1,2},{2,1},{3,4},{4,3},{5,6},{6,5},{7,8},{8,7},{9,10},{10,9},{11,... | collective-permute-start | bytes 786440 | tf_op jit(solution)/shard_map/ppermute | solution.py:33
  3.9 0.7 %collective-permute-start.2 = (bf16[1024,128]{1,0:T(8,128)(2,1)}, bf16[1024,128]{1,0:T(8,128)(2,1)S(1)}, u32[]{:S(2)}, u32[]{:S(2)}) collective-permute-start(bf16[1024,128]{1,0:T(8,128)(2,1)} %bitcast.30), channel_id=1, source_target_pairs={{1,2},{2,1},{3,4},{4,3},{5,6},{6,5},{7,8},{8,7},{9,10},{10,9},{11,... | collective-permute-start | bytes 786440 | tf_op jit(solution)/shard_map/ppermute | solution.py:33
  4.5 5.8 %collective-permute-start.3 = (bf16[1024,128]{1,0:T(8,128)(2,1)}, bf16[1024,128]{1,0:T(8,128)(2,1)S(1)}, u32[]{:S(2)}, u32[]{:S(2)}) collective-permute-start(bf16[1024,128]{1,0:T(8,128)(2,1)} %bitcast.35), channel_id=1, source_target_pairs={{0,1},{1,0},{2,3},{3,2},{4,5},{5,4},{6,7},{7,6},{8,9},{9,8},{10,11... | collective-permute-start | bytes 786440 | tf_op jit(solution)/shard_map/ppermute | solution.py:33
  10.4 0.1 pad_add_fusion.place
  10.5 0.9 %copy-done.1 = bf16[1,1,32,32,128]{4,3,2,1,0:T(8,128)(2,1)S(1)} copy-done((bf16[1,1,32,32,128]{4,3,2,1,0:T(8,128)(2,1)S(1)}, bf16[1,1,32,32,128]{4,3,2,1,0:T(8,128)(2,1)}, u32[]{:S(2)}) %copy-start.1) | copy-done | bytes 262168
  11.4 0.9 %copy-done.3 = bf16[1,1,32,32,128]{4,3,2,1,0:T(8,128)(2,1)S(1)} copy-done((bf16[1,1,32,32,128]{4,3,2,1,0:T(8,128)(2,1)S(1)}, bf16[1,1,32,32,128]{4,3,2,1,0:T(8,128)(2,1)}, u32[]{:S(2)}) %copy-start.3) | copy-done | bytes 262168
  12.4 2.0 %centre.1 = (f32[4,3,16,384]{3,2,1,0:T(8,128)S(1)}, f32[4,3,16,384]{3,2,1,0:T(8,128)S(1)}, bf16[384,1024]{1,0:T(8,128)(2,1)S(1)}) custom-call(s32[4]{0:T(128)S(1)} %pad_add_fusion.place, bf16[1024,128]{1,0:T(8,128)(2,1)S(1)} %bitcast.31, bf16[1024,128]{1,0:T(8,128)(2,1)S(1)} %bitcast.36), custom_call_target="tpu_custom_call" | custom-call | flops 1048576 | bytes 65536 | tf_op jit(solution)/shard_map/centre/pallas_call | solution.py:185
  14.4 2.5 %side.1 = (f32[4,6,16,384]{3,2,1,0:T(8,128)S(1)}, f32[4,6,16,384]{3,2,1,0:T(8,128)S(1)}) custom-call(s32[4]{0:T(128)S(1)} %pad_add_fusion.place, bf16[1024,128]{1,0:T(8,128)(2,1)S(1)} %bitcast.32, bf16[1024,128]{1,0:T(8,128)(2,1)S(1)} %collective-permute-done.near_vol.partner_plane, bf16[1024,128]{1,0:T(8,128)(2,1)S(1)} %collective-permute-done.1.near_cot.other_plane, ...), custom_call_target="tpu_custom_call" | custom-call | flops 1048576 | bytes 65536 | tf_op jit(solution)/shard_map/side/pallas_call | solution.py:202
  16.9 1.6 %collective-permute-start.4 = (f32[4,6,16,384]{3,2,1,0:T(8,128)S(1)}, f32[4,6,16,384]{3,2,1,0:T(8,128)S(1)}, u32[]{:S(2)}, u32[]{:S(2)}) collective-permute-start(f32[4,6,16,384]{3,2,1,0:T(8,128)S(1)} %get-tuple-element.18), channel_id=1, source_target_pairs={{0,32},{1,33},{2,34},{3,35},{4,36},{5,37},{6,38},{7,39},{8,40},{9,... | collective-permute-start | bytes 1769480 | tf_op jit(solution)/shard_map/ppermute | solution.py:33
  18.6 1.6 %collective-permute-done.4 = f32[4,6,16,384]{3,2,1,0:T(8,128)S(1)} collective-permute-done((f32[4,6,16,384]{3,2,1,0:T(8,128)S(1)}, f32[4,6,16,384]{3,2,1,0:T(8,128)S(1)}, u32[]{:S(2)}, u32[]{:S(2)}) %collective-permute-start.4) | collective-permute-done | bytes 589856 | tf_op jit(solution)/shard_map/ppermute | solution.py:33
  20.3 0.1 abs_reduce_fusion
  20.4 0.1 multiply_convert_fusion
  20.5 0.1 broadcast_in_dim.2
  20.7 7.1 %collective-permute-start.7 = (f16[7,16,384]{2,1,0:T(8,128)(2,1)S(1)}, f16[7,16,384]{2,1,0:T(8,128)(2,1)S(1)}, u32[]{:S(2)}, u32[]{:S(2)}) collective-permute-start(f16[7,16,384]{2,1,0:T(8,128)(2,1)S(1)} %get-tuple-element.24), channel_id=1, source_target_pairs={{0,24},{1,25},{2,26},{3,27},{4,28},{5,29},{6,30},{7,31},{8,16},{9,... | collective-permute-start | bytes 258056 | tf_op jit(solution)/shard_map/ppermute | solution.py:33
  27.8 0.2 collective-permute-start.6
  28.0 0.5 collective-permute-start.5
  28.5 3.0 %grad_volume.1 = bf16[1024,128]{1,0:T(8,128)(2,1)} custom-call(s32[4]{0:T(128)S(1)} %pad_add_fusion.place, bf16[27,128,128]{2,1,0:T(8,128)(2,1)S(1)} %copy-done, bf16[1024,128]{1,0:T(8,128)(2,1)S(1)} %collective-permute-done.3.partner_plane, bf16[1024,128]{1,0:T(8,128)(2,1)S(1)} %bitcast.37, bf16[1024,128]{1,0:T(8,128)(2,1)S(1)} %collective-permute-done.1.near_cot.other_plane), custom_call_target="tpu_custom_call" | custom-call | flops 1048576 | bytes 65536 | tf_op jit(solution)/shard_map/grad_volume/pallas_call | solution.py:220
  31.5 1.1 %collective-permute-done.6 = f16[7,16,384]{2,1,0:T(8,128)(2,1)S(1)} collective-permute-done((f16[7,16,384]{2,1,0:T(8,128)(2,1)S(1)}, f16[7,16,384]{2,1,0:T(8,128)(2,1)S(1)}, u32[]{:S(2)}, u32[]{:S(2)}) %collective-permute-start.6) | collective-permute-done | bytes 86048 | tf_op jit(solution)/shard_map/ppermute | solution.py:33
  32.8 4.6 %collective-permute-start.10 = (f32[24,384]{1,0:T(8,128)S(1)}, f32[24,384]{1,0:T(8,128)S(1)}, u32[]{:S(2)}, u32[]{:S(2)}) collective-permute-start(f32[24,384]{1,0:T(8,128)S(1)} %reshape_squeeze.14), channel_id=1, source_target_pairs={{0,4},{1,36},{2,6},{3,38},{4,0},{5,32},{6,2},{7,34},{8,12},{9,44},... | collective-permute-start | bytes 110600 | tf_op jit(solution)/shard_map/ppermute | solution.py:33
  37.4 0.2 collective-permute-start.11
  37.7 4.9 %collective-permute-start.8 = (f32[24,384]{1,0:T(8,128)S(1)}, f32[24,384]{1,0:T(8,128)S(1)}, u32[]{:S(2)}, u32[]{:S(2)}) collective-permute-start(f32[24,384]{1,0:T(8,128)S(1)} %reshape_squeeze.12), channel_id=1, source_target_pairs={{0,0},{1,32},{2,2},{3,34},{4,4},{5,36},{6,6},{7,38},{8,8},{9,40},{... | collective-permute-start | bytes 110600 | tf_op jit(solution)/shard_map/ppermute | solution.py:33
  42.6 0.6 %collective-permute-start.9 = (f32[24,384]{1,0:T(8,128)S(1)}, f32[24,384]{1,0:T(8,128)S(1)}, u32[]{:S(2)}, u32[]{:S(2)}) collective-permute-start(f32[24,384]{1,0:T(8,128)S(1)} %reshape_squeeze.13), channel_id=1, source_target_pairs={{0,2},{1,34},{2,0},{3,32},{4,6},{5,38},{6,4},{7,36},{8,10},{9,42},... | collective-permute-start | bytes 110600 | tf_op jit(solution)/shard_map/ppermute | solution.py:33
  43.2 3.0 %response.1 = bf16[1024,128]{1,0:T(8,128)(2,1)} custom-call(s32[4]{0:T(128)S(1)} %pad_add_fusion.place, bf16[27,128,128]{2,1,0:T(8,128)(2,1)S(1)} %copy-done, bf16[1024,128]{1,0:T(8,128)(2,1)S(1)} %collective-permute-done.near_vol.partner_plane, bf16[1024,128]{1,0:T(8,128)(2,1)S(1)} %bitcast.33, bf16[1024,128]{1,0:T(8,128)(2,1)S(1)} %collective-permute-done.2.other_plane), custom_call_target="tpu_custom_call" | custom-call | flops 1048576 | bytes 65536 | tf_op jit(solution)/shard_map/response/pallas_call | solution.py:220
  46.3 1.6 %collective-permute-done.9 = f32[24,384]{1,0:T(8,128)S(1)} collective-permute-done((f32[24,384]{1,0:T(8,128)S(1)}, f32[24,384]{1,0:T(8,128)S(1)}, u32[]{:S(2)}, u32[]{:S(2)}) %collective-permute-start.9) | collective-permute-done | bytes 36896 | tf_op jit(solution)/shard_map/ppermute | solution.py:33
  47.9 1.4 %collective-permute-start.12 = (f32[24,384]{1,0:T(8,128)S(1)}, f32[24,384]{1,0:T(8,128)S(1)}, u32[]{:S(2)}, u32[]{:S(2)}) collective-permute-start(f32[24,384]{1,0:T(8,128)S(1)} %add_add_fusion), channel_id=1, source_target_pairs={{0,64},{1,65},{2,66},{3,67},{4,68},{5,69},{6,70},{7,71},{8,72},{9,... | collective-permute-start | bytes 110600 | tf_op jit(solution)/shard_map/ppermute | solution.py:33
  49.3 1.5 %collective-permute-done.12 = f32[24,384]{1,0:T(8,128)S(1)} collective-permute-done((f32[24,384]{1,0:T(8,128)S(1)}, f32[24,384]{1,0:T(8,128)S(1)}, u32[]{:S(2)}, u32[]{:S(2)}) %collective-permute-start.12) | collective-permute-done | bytes 36896 | tf_op jit(solution)/shard_map/ppermute | solution.py:33
  50.8 2.7 %collective-permute-start.13 = (f32[24,384]{1,0:T(8,128)S(1)}, f32[24,384]{1,0:T(8,128)S(1)}, u32[]{:S(2)}, u32[]{:S(2)}) collective-permute-start(f32[24,384]{1,0:T(8,128)S(1)} %add.47), channel_id=1, source_target_pairs={{0,192},{1,193},{2,194},{3,195},{4,196},{5,197},{6,198},{7,199},{8... | collective-permute-start | bytes 110600 | tf_op jit(solution)/shard_map/ppermute | solution.py:33
  53.5 1.4 %collective-permute-done.13 = f32[24,384]{1,0:T(8,128)S(1)} collective-permute-done((f32[24,384]{1,0:T(8,128)S(1)}, f32[24,384]{1,0:T(8,128)S(1)}, u32[]{:S(2)}, u32[]{:S(2)}) %collective-permute-start.13) | collective-permute-done | bytes 36896 | tf_op jit(solution)/shard_map/ppermute | solution.py:33
  55.0 0.4 collective-permute-start.14
  55.3 0.9 %collective-permute-done.14 = f32[24,384]{1,0:T(8,128)S(1)} collective-permute-done((f32[24,384]{1,0:T(8,128)S(1)}, f32[24,384]{1,0:T(8,128)S(1)}, u32[]{:S(2)}, u32[]{:S(2)}) %collective-permute-start.14) | collective-permute-done | bytes 36896 | tf_op jit(solution)/shard_map/ppermute | solution.py:33
  56.3 0.6 %copy.6 = f32[4,3,3,3,128]{4,0,3,2,1:T(4,128)} copy(f32[4,3,3,3,128]{4,2,0,3,1:T(4,128)S(1)} %fusion.7) | data formatting | bytes 110592 | tf_op jit(solution)/shard_map/mul | solution.py:284
  (37 shorter events, 0.5 us)
Async XLA Ops:
  0.6 13.8 %collective-permute-start = (bf16[1024,128]{1,0:T(8,128)(2,1)}, bf16[1024,128]{1,0:T(8,128)(2,1)S(1)}, u32[]{:S(2)}, u32[]{:S(2)}) collective-permute-start(bf16[1024,128]{1,0:T(8,128)(2,1)} %bitcast.29), channel_id=1, source_target_pairs={{0,1},{1,0},{2,3},{3,2},{4,5},{5,4},{6,7},{7,6},{8,9},{9,8},{10,11... | collective-permute-start | bytes 786440 | tf_op jit(solution)/shard_map/ppermute | solution.py:33
  3.2 11.2 %collective-permute-start.1 = (bf16[1024,128]{1,0:T(8,128)(2,1)}, bf16[1024,128]{1,0:T(8,128)(2,1)S(1)}, u32[]{:S(2)}, u32[]{:S(2)}) collective-permute-start(bf16[1024,128]{1,0:T(8,128)(2,1)} %bitcast.34), channel_id=1, source_target_pairs={{1,2},{2,1},{3,4},{4,3},{5,6},{6,5},{7,8},{8,7},{9,10},{10,9},{11,... | collective-permute-start | bytes 786440 | tf_op jit(solution)/shard_map/ppermute | solution.py:33
  3.9 13.1 %collective-permute-start.2 = (bf16[1024,128]{1,0:T(8,128)(2,1)}, bf16[1024,128]{1,0:T(8,128)(2,1)S(1)}, u32[]{:S(2)}, u32[]{:S(2)}) collective-permute-start(bf16[1024,128]{1,0:T(8,128)(2,1)} %bitcast.30), channel_id=1, source_target_pairs={{1,2},{2,1},{3,4},{4,3},{5,6},{6,5},{7,8},{8,7},{9,10},{10,9},{11,... | collective-permute-start | bytes 786440 | tf_op jit(solution)/shard_map/ppermute | solution.py:33
  4.5 12.4 %collective-permute-start.3 = (bf16[1024,128]{1,0:T(8,128)(2,1)}, bf16[1024,128]{1,0:T(8,128)(2,1)S(1)}, u32[]{:S(2)}, u32[]{:S(2)}) collective-permute-start(bf16[1024,128]{1,0:T(8,128)(2,1)} %bitcast.35), channel_id=1, source_target_pairs={{0,1},{1,0},{2,3},{3,2},{4,5},{5,4},{6,7},{7,6},{8,9},{9,8},{10,11... | collective-permute-start | bytes 786440 | tf_op jit(solution)/shard_map/ppermute | solution.py:33
  10.5 1.0 %copy-start.1 = (bf16[1,1,32,32,128]{4,3,2,1,0:T(8,128)(2,1)S(1)}, bf16[1,1,32,32,128]{4,3,2,1,0:T(8,128)(2,1)}, u32[]{:S(2)}) copy-start(bf16[1,1,32,32,128]{4,3,2,1,0:T(8,128)(2,1)} %param.3) | copy-start | bytes 786436
  11.4 0.9 %copy-start.3 = (bf16[1,1,32,32,128]{4,3,2,1,0:T(8,128)(2,1)S(1)}, bf16[1,1,32,32,128]{4,3,2,1,0:T(8,128)(2,1)}, u32[]{:S(2)}) copy-start(bf16[1,1,32,32,128]{4,3,2,1,0:T(8,128)(2,1)} %param.5) | copy-start | bytes 786436
  12.4 2.1 %copy-start.2 = (bf16[1,1,32,32,128]{4,3,2,1,0:T(8,128)(2,1)S(1)}, bf16[1,1,32,32,128]{4,3,2,1,0:T(8,128)(2,1)}, u32[]{:S(2)}) copy-start(bf16[1,1,32,32,128]{4,3,2,1,0:T(8,128)(2,1)} %param.3) | copy-start | bytes 786436
  16.9 3.3 %collective-permute-start.4 = (f32[4,6,16,384]{3,2,1,0:T(8,128)S(1)}, f32[4,6,16,384]{3,2,1,0:T(8,128)S(1)}, u32[]{:S(2)}, u32[]{:S(2)}) collective-permute-start(f32[4,6,16,384]{3,2,1,0:T(8,128)S(1)} %get-tuple-element.18), channel_id=1, source_target_pairs={{0,32},{1,33},{2,34},{3,35},{4,36},{5,37},{6,38},{7,39},{8,40},{9,... | collective-permute-start | bytes 1769480 | tf_op jit(solution)/shard_map/ppermute | solution.py:33
  20.3 8.2 %copy-start = (bf16[27,128,128]{2,1,0:T(8,128)(2,1)S(1)}, bf16[27,128,128]{2,1,0:T(8,128)(2,1)}, u32[]{:S(2)}) copy-start(bf16[27,128,128]{2,1,0:T(8,128)(2,1)} %weights.3) | copy-start | bytes 2654212
  20.7 10.8 %collective-permute-start.7 = (f16[7,16,384]{2,1,0:T(8,128)(2,1)S(1)}, f16[7,16,384]{2,1,0:T(8,128)(2,1)S(1)}, u32[]{:S(2)}, u32[]{:S(2)}) collective-permute-start(f16[7,16,384]{2,1,0:T(8,128)(2,1)S(1)} %get-tuple-element.24), channel_id=1, source_target_pairs={{0,24},{1,25},{2,26},{3,27},{4,28},{5,29},{6,30},{7,31},{8,16},{9,... | collective-permute-start | bytes 258056 | tf_op jit(solution)/shard_map/ppermute | solution.py:33
  27.8 4.8 %collective-permute-start.6 = (f16[7,16,384]{2,1,0:T(8,128)(2,1)S(1)}, f16[7,16,384]{2,1,0:T(8,128)(2,1)S(1)}, u32[]{:S(2)}, u32[]{:S(2)}) collective-permute-start(f16[7,16,384]{2,1,0:T(8,128)(2,1)S(1)} %get-tuple-element.25), channel_id=1, source_target_pairs={{0,16},{1,17},{2,18},{3,19},{4,20},{5,21},{6,22},{7,23},{8,24},{9,... | collective-permute-start | bytes 258056 | tf_op jit(solution)/shard_map/ppermute | solution.py:33
  28.0 4.6 %collective-permute-start.5 = (f16[7,16,384]{2,1,0:T(8,128)(2,1)S(1)}, f16[7,16,384]{2,1,0:T(8,128)(2,1)S(1)}, u32[]{:S(2)}, u32[]{:S(2)}) collective-permute-start(f16[7,16,384]{2,1,0:T(8,128)(2,1)S(1)} %get-tuple-element.23), channel_id=1, source_target_pairs={{0,8},{1,9},{2,10},{3,11},{4,12},{5,13},{6,14},{7,15},{8,0},{9,1},... | collective-permute-start | bytes 258056 | tf_op jit(solution)/shard_map/ppermute | solution.py:33
  32.8 13.4 %collective-permute-start.10 = (f32[24,384]{1,0:T(8,128)S(1)}, f32[24,384]{1,0:T(8,128)S(1)}, u32[]{:S(2)}, u32[]{:S(2)}) collective-permute-start(f32[24,384]{1,0:T(8,128)S(1)} %reshape_squeeze.14), channel_id=1, source_target_pairs={{0,4},{1,36},{2,6},{3,38},{4,0},{5,32},{6,2},{7,34},{8,12},{9,44},... | collective-permute-start | bytes 110600 | tf_op jit(solution)/shard_map/ppermute | solution.py:33
  37.4 8.8 %collective-permute-start.11 = (f32[24,384]{1,0:T(8,128)S(1)}, f32[24,384]{1,0:T(8,128)S(1)}, u32[]{:S(2)}, u32[]{:S(2)}) collective-permute-start(f32[24,384]{1,0:T(8,128)S(1)} %reshape_squeeze.15), channel_id=1, source_target_pairs={{0,6},{1,38},{2,4},{3,36},{4,2},{5,34},{6,0},{7,32},{8,14},{9,46},... | collective-permute-start | bytes 110600 | tf_op jit(solution)/shard_map/ppermute | solution.py:33
  37.7 8.6 %collective-permute-start.8 = (f32[24,384]{1,0:T(8,128)S(1)}, f32[24,384]{1,0:T(8,128)S(1)}, u32[]{:S(2)}, u32[]{:S(2)}) collective-permute-start(f32[24,384]{1,0:T(8,128)S(1)} %reshape_squeeze.12), channel_id=1, source_target_pairs={{0,0},{1,32},{2,2},{3,34},{4,4},{5,36},{6,6},{7,38},{8,8},{9,40},{... | collective-permute-start | bytes 110600 | tf_op jit(solution)/shard_map/ppermute | solution.py:33
  42.6 5.3 %collective-permute-start.9 = (f32[24,384]{1,0:T(8,128)S(1)}, f32[24,384]{1,0:T(8,128)S(1)}, u32[]{:S(2)}, u32[]{:S(2)}) collective-permute-start(f32[24,384]{1,0:T(8,128)S(1)} %reshape_squeeze.13), channel_id=1, source_target_pairs={{0,2},{1,34},{2,0},{3,32},{4,6},{5,38},{6,4},{7,36},{8,10},{9,42},... | collective-permute-start | bytes 110600 | tf_op jit(solution)/shard_map/ppermute | solution.py:33
  47.9 2.9 %collective-permute-start.12 = (f32[24,384]{1,0:T(8,128)S(1)}, f32[24,384]{1,0:T(8,128)S(1)}, u32[]{:S(2)}, u32[]{:S(2)}) collective-permute-start(f32[24,384]{1,0:T(8,128)S(1)} %add_add_fusion), channel_id=1, source_target_pairs={{0,64},{1,65},{2,66},{3,67},{4,68},{5,69},{6,70},{7,71},{8,72},{9,... | collective-permute-start | bytes 110600 | tf_op jit(solution)/shard_map/ppermute | solution.py:33
  50.8 4.1 %collective-permute-start.13 = (f32[24,384]{1,0:T(8,128)S(1)}, f32[24,384]{1,0:T(8,128)S(1)}, u32[]{:S(2)}, u32[]{:S(2)}) collective-permute-start(f32[24,384]{1,0:T(8,128)S(1)} %add.47), channel_id=1, source_target_pairs={{0,192},{1,193},{2,194},{3,195},{4,196},{5,197},{6,198},{7,199},{8... | collective-permute-start | bytes 110600 | tf_op jit(solution)/shard_map/ppermute | solution.py:33
  55.0 1.2 %collective-permute-start.14 = (f32[24,384]{1,0:T(8,128)S(1)}, f32[24,384]{1,0:T(8,128)S(1)}, u32[]{:S(2)}, u32[]{:S(2)}) collective-permute-start(f32[24,384]{1,0:T(8,128)S(1)} %add.48), channel_id=1, source_target_pairs={{0,32},{1,33},{2,34},{3,35},{4,36},{5,37},{6,38},{7,39},{8,40},{9,... | collective-permute-start | bytes 110600 | tf_op jit(solution)/shard_map/ppermute | solution.py:33

commit v3 on v2

--- a/solution.py
+++ b/solution.py
@@ -88,8 +88,9 @@
     for s in range(4):
         for c in range(3):
             start = c * C + s * 16
-            keep[s, slot + c] = total[start : start + 16]
-            send[s, slot + c] = total[start + 64 : start + 80]
+            lanes = slice((slot + c) * 3 * C, (slot + c + 1) * 3 * C)
+            keep[s, :, lanes] = total[start : start + 16]
+            send[s, :, lanes] = total[start + 64 : start + 80]
 
 
 def centre_kernel(place, vol, cot, keep, send, rows, padded, cots, sems):
@@ -117,8 +118,8 @@
     ]
     for copy in copies:
         copy.start()
-    keep[:, 0:3] = keep0[...]
-    send[:, 0:3] = send0[...]
+    keep[:, :, 0 : 9 * C] = keep0[...]
+    send[:, :, 0 : 9 * C] = send0[...]
     zero_edges(padded.at[0])
     zero_edges(padded.at[1])
     order = row_order(place)
@@ -174,8 +175,8 @@
         out[pl.ds(start, 1024), :] = (mid + low + high).astype(BF16)
 
 
-HALF = jax.ShapeDtypeStruct((4, 3, 16, 3 * C), F32)
-WHOLE = jax.ShapeDtypeStruct((4, 6, 16, 3 * C), F32)
+HALF = jax.ShapeDtypeStruct((4, 16, 9 * C), F32)
+WHOLE = jax.ShapeDtypeStruct((4, 16, 18 * C), F32)
 ROWS = jax.ShapeDtypeStruct((3 * C, CELLS), BF16)
 COST = pl.CostEstimate(flops=1 << 20, bytes_accessed=1 << 16, transcendentals=0)
 PARAMS = pltpu.CompilerParams(vmem_limit_bytes=32 * 1024 * 1024)
@@ -254,18 +255,18 @@
     total = keep + move(after(send, other_vol, partner_cot), swap)
 
     away = total[1:]
-    peak = jnp.max(jnp.abs(away), axis=(1, 3), keepdims=True)
-    power = jnp.clip(jnp.ceil(jnp.log2(peak)), -100.0, 100.0)
+    peak = jnp.max(jnp.abs(away), axis=2, keepdims=True)
+    power = jnp.clip(jnp.ceil(jnp.log2(peak)), -126.0, 100.0)
     scaled = (away * jnp.exp2(-power)).astype(jnp.float16)
-    powers = jnp.broadcast_to(power, (3, 1, 16, 3 * C)).astype(jnp.float16)
-    packed = jnp.concatenate([scaled, powers], axis=1)
+    powers = jnp.broadcast_to(power, (3, 16, C)).astype(jnp.float16)
+    packed = jnp.concatenate([scaled, powers], axis=2)
     parts = [move(packed[s - 1], across_x(s)) for s in range(1, 4)]
-    parts = [p[:6].astype(F32) * jnp.exp2(p[6:].astype(F32)) for p in parts]
+    parts = [p[:, : 18 * C].astype(F32) * jnp.exp2(p[:, 18 * C : 18 * C + 1].astype(F32)) for p in parts]
     grad_volume = conv(True, after(place, total), kernel, partner_cot, cot, other_cot)
     total = total[0] + parts[0] + (parts[1] + parts[2])
     total = after(total, grad_volume)
 
-    pieces = [total.reshape(6, 4, 4, 3 * C)[:, t].reshape(24, 3 * C) for t in range(4)]
+    pieces = [total[4 * t : 4 * t + 4] for t in range(4)]
 
     def to_owner(t):
         return lambda y, c, s: (y, s & 1, ((s ^ (2 * t)) & ~1) | c)
@@ -275,13 +276,13 @@
     total = (parts[0] + parts[1]) + (parts[2] + parts[3])
     total = after(total, response)
 
-    for s in (1, 3):
-        total = total + move(total, across_y(s))
+    total = total + move(total, across_y(1))
+    total = total + move(total, across_y(3))
     twin = move(total, swap)
-    from_even = jnp.where(core == 0, total, twin).reshape(2, 3, 4, 3, C)
-    from_odd = jnp.where(core == 0, twin, total).reshape(2, 3, 4, 3, C)
-    taps = jnp.stack([from_odd[1], from_even[0] + from_odd[0], from_even[1]])
-    grad_kernel = (taps.transpose(2, 0, 3, 1, 4) * scale).reshape(4, 27, C)
+    from_even = jnp.where(core == 0, total, twin).reshape(4, 2, 3, 3, C)
+    from_odd = jnp.where(core == 0, twin, total).reshape(4, 2, 3, 3, C)
+    taps = jnp.stack([from_odd[:, 1], from_even[:, 0] + from_odd[:, 0], from_even[:, 1]], axis=1)
+    grad_kernel = (taps.transpose(0, 1, 3, 2, 4) * scale).reshape(4, 27, C)
     return (response.reshape(volume.shape), grad_volume.reshape(volume.shape), grad_kernel)
 
 

time: 57.1 us -> 57.1 us (level)
  transfers between devices with their start and end apart: 15 -> 15, of which waited for: 6 -> 6; matrix products, arithmetic and copies ran while one was open for 0% -> 1% of each run, Pallas kernels for 18% -> 18%
where the time goes in v3:
time: 57.1 us; the launch traced here: 56.9 us
  starting transfers between devices  33.8 us (59%)
  Pallas kernels  10.5 us (18%)
  waiting for transfers between devices  8.15 us (14%)
  local copies, waits for them, and re-layouts  2.64 us (5%)
  other arithmetic  1.02 us (2%)
  between operations  0.85 us (1%)
    ppermute x15, starting transfers between devices, move(): return lax.ppermute(array, AXES, perm)  33.8 us
    ppermute x15, waiting for transfers between devices, move(): return lax.ppermute(array, AXES, perm)  8.15 us
    pallas_call x2, Pallas kernels, conv(): pl.pallas_call(functools.partial(conv_kernel, backward), out_shape=jax.Sh...  5.98 us
    pallas_call x1, Pallas kernels, side(): pl.pallas_call(side_kernel, out_shape=(WHOLE, WHOLE), in_specs=[SMEM, HBM...  2.48 us
    pallas_call x1, Pallas kernels, centre(): pl.pallas_call(centre_kernel, out_shape=(HALF, HALF, ROWS), in_specs=[SME...  2.02 us
    unnamed x8, local copies, waits for them, and re-layouts  1.91 us
  transfers between devices with their start and end apart: 15, of which 6 were waited for; matrix products, arithmetic and copies ran while one was open for 1% of the time, Pallas kernels for 18%

profile of v3, /device:TPU:1, one launch (start us, length us, event | category | flops | bytes accessed | tf_op | source)
XLA Modules:
  0.0 56.9 jit_solution(4666465730696122777)
XLA Ops:
  0.6 2.6 %collective-permute-start = (bf16[1024,128]{1,0:T(8,128)(2,1)}, bf16[1024,128]{1,0:T(8,128)(2,1)S(1)}, u32[]{:S(2)}, u32[]{:S(2)}) collective-permute-start(bf16[1024,128]{1,0:T(8,128)(2,1)} %bitcast.25), channel_id=1, source_target_pairs={{0,1},{1,0},{2,3},{3,2},{4,5},{5,4},{6,7},{7,6},{8,9},{9,8},{10,11... | collective-permute-start | bytes 786440 | tf_op jit(solution)/shard_map/ppermute | solution.py:33
  3.2 0.7 %collective-permute-start.1 = (bf16[1024,128]{1,0:T(8,128)(2,1)}, bf16[1024,128]{1,0:T(8,128)(2,1)S(1)}, u32[]{:S(2)}, u32[]{:S(2)}) collective-permute-start(bf16[1024,128]{1,0:T(8,128)(2,1)} %bitcast.30), channel_id=1, source_target_pairs={{1,2},{2,1},{3,4},{4,3},{5,6},{6,5},{7,8},{8,7},{9,10},{10,9},{11,... | collective-permute-start | bytes 786440 | tf_op jit(solution)/shard_map/ppermute | solution.py:33
  3.9 0.7 %collective-permute-start.2 = (bf16[1024,128]{1,0:T(8,128)(2,1)}, bf16[1024,128]{1,0:T(8,128)(2,1)S(1)}, u32[]{:S(2)}, u32[]{:S(2)}) collective-permute-start(bf16[1024,128]{1,0:T(8,128)(2,1)} %bitcast.26), channel_id=1, source_target_pairs={{1,2},{2,1},{3,4},{4,3},{5,6},{6,5},{7,8},{8,7},{9,10},{10,9},{11,... | collective-permute-start | bytes 786440 | tf_op jit(solution)/shard_map/ppermute | solution.py:33
  4.5 5.8 %collective-permute-start.3 = (bf16[1024,128]{1,0:T(8,128)(2,1)}, bf16[1024,128]{1,0:T(8,128)(2,1)S(1)}, u32[]{:S(2)}, u32[]{:S(2)}) collective-permute-start(bf16[1024,128]{1,0:T(8,128)(2,1)} %bitcast.31), channel_id=1, source_target_pairs={{0,1},{1,0},{2,3},{3,2},{4,5},{5,4},{6,7},{7,6},{8,9},{9,8},{10,11... | collective-permute-start | bytes 786440 | tf_op jit(solution)/shard_map/ppermute | solution.py:33
  10.5 0.9 %copy-done.1 = bf16[1,1,32,32,128]{4,3,2,1,0:T(8,128)(2,1)S(1)} copy-done((bf16[1,1,32,32,128]{4,3,2,1,0:T(8,128)(2,1)S(1)}, bf16[1,1,32,32,128]{4,3,2,1,0:T(8,128)(2,1)}, u32[]{:S(2)}) %copy-start.1) | copy-done | bytes 262168
  11.4 0.9 %copy-done.3 = bf16[1,1,32,32,128]{4,3,2,1,0:T(8,128)(2,1)S(1)} copy-done((bf16[1,1,32,32,128]{4,3,2,1,0:T(8,128)(2,1)S(1)}, bf16[1,1,32,32,128]{4,3,2,1,0:T(8,128)(2,1)}, u32[]{:S(2)}) %copy-start.3) | copy-done | bytes 262168
  12.4 2.0 %centre.1 = (f32[4,16,1152]{2,1,0:T(8,128)S(1)}, f32[4,16,1152]{2,1,0:T(8,128)S(1)}, bf16[384,1024]{1,0:T(8,128)(2,1)S(1)}) custom-call(s32[4]{0:T(128)S(1)} %pad_add_fusion.place, bf16[1024,128]{1,0:T(8,128)(2,1)S(1)} %bitcast.27, bf16[1024,128]{1,0:T(8,128)(2,1)S(1)} %bitcast.32), custom_call_target="tpu_custom_call" | custom-call | flops 1048576 | bytes 65536 | tf_op jit(solution)/shard_map/centre/pallas_call | solution.py:186
  14.4 2.5 %side.1 = (f32[4,16,2304]{2,1,0:T(8,128)S(1)}, f32[4,16,2304]{2,1,0:T(8,128)S(1)}) custom-call(s32[4]{0:T(128)S(1)} %pad_add_fusion.place, bf16[1024,128]{1,0:T(8,128)(2,1)S(1)} %bitcast.28, bf16[1024,128]{1,0:T(8,128)(2,1)S(1)} %collective-permute-done.near_vol.partner_plane, bf16[1024,128]{1,0:T(8,128)(2,1)S(1)} %collective-permute-done.1.near_cot.other_plane, ...), custom_call_target="tpu_custom_call" | custom-call | flops 1048576 | bytes 65536 | tf_op jit(solution)/shard_map/side/pallas_call | solution.py:203
  16.9 1.6 %collective-permute-start.4 = (f32[4,16,2304]{2,1,0:T(8,128)S(1)}, f32[4,16,2304]{2,1,0:T(8,128)S(1)}, u32[]{:S(2)}, u32[]{:S(2)}) collective-permute-start(f32[4,16,2304]{2,1,0:T(8,128)S(1)} %get-tuple-element.18), channel_id=1, source_target_pairs={{0,32},{1,33},{2,34},{3,35},{4,36},{5,37},{6,38},{7,39},{8,40},{9,... | collective-permute-start | bytes 1769480 | tf_op jit(solution)/shard_map/ppermute | solution.py:33
  18.6 1.6 %collective-permute-done.4 = f32[4,16,2304]{2,1,0:T(8,128)S(1)} collective-permute-done((f32[4,16,2304]{2,1,0:T(8,128)S(1)}, f32[4,16,2304]{2,1,0:T(8,128)S(1)}, u32[]{:S(2)}, u32[]{:S(2)}) %collective-permute-start.4) | collective-permute-done | bytes 589856 | tf_op jit(solution)/shard_map/ppermute | solution.py:33
  20.4 0.1 multiply_convert_fusion
  20.7 7.1 %collective-permute-start.7 = (f16[16,2432]{1,0:T(8,128)(2,1)S(1)}, f16[16,2432]{1,0:T(8,128)(2,1)S(1)}, u32[]{:S(2)}, u32[]{:S(2)}) collective-permute-start(f16[16,2432]{1,0:T(8,128)(2,1)S(1)} %get-tuple-element.24), channel_id=1, source_target_pairs={{0,24},{1,25},{2,26},{3,27},{4,28},{5,29},{6,30},{7,31},{8,16},{9,... | collective-permute-start | bytes 233480 | tf_op jit(solution)/shard_map/ppermute | solution.py:33
  27.8 0.2 collective-permute-start.6
  28.0 0.5 collective-permute-start.5
  28.5 3.0 %grad_volume.1 = bf16[1024,128]{1,0:T(8,128)(2,1)} custom-call(s32[4]{0:T(128)S(1)} %pad_add_fusion.place, bf16[27,128,128]{2,1,0:T(8,128)(2,1)S(1)} %copy-done, bf16[1024,128]{1,0:T(8,128)(2,1)S(1)} %collective-permute-done.3.partner_plane, bf16[1024,128]{1,0:T(8,128)(2,1)S(1)} %bitcast.33, bf16[1024,128]{1,0:T(8,128)(2,1)S(1)} %collective-permute-done.1.near_cot.other_plane), custom_call_target="tpu_custom_call" | custom-call | flops 1048576 | bytes 65536 | tf_op jit(solution)/shard_map/grad_volume/pallas_call | solution.py:221
  31.5 0.1 exponential_reduce_fusion
  31.6 0.9 %collective-permute-done.6 = f16[16,2432]{1,0:T(8,128)(2,1)S(1)} collective-permute-done((f16[16,2432]{1,0:T(8,128)(2,1)S(1)}, f16[16,2432]{1,0:T(8,128)(2,1)S(1)}, u32[]{:S(2)}, u32[]{:S(2)}) %collective-permute-start.6) | collective-permute-done | bytes 77856 | tf_op jit(solution)/shard_map/ppermute | solution.py:33
  32.5 0.1 exponential_reduce_fusion.1
  32.7 0.1 exponential_reduce_fusion.2
  32.8 0.1 fusion.1
  33.0 4.4 %collective-permute-start.10 = (f32[4,2304]{1,0:T(4,128)S(1)}, f32[4,2304]{1,0:T(4,128)S(1)}, u32[]{:S(2)}, u32[]{:S(2)}) collective-permute-start(f32[4,2304]{1,0:T(4,128)S(1)} %get-tuple-element.28), channel_id=1, source_target_pairs={{0,4},{1,36},{2,6},{3,38},{4,0},{5,32},{6,2},{7,34},{8,12},{9,44},... | collective-permute-start | bytes 110600 | tf_op jit(solution)/shard_map/ppermute | solution.py:33
  37.5 4.9 %collective-permute-start.8 = (f32[4,2304]{1,0:T(4,128)S(1)}, f32[4,2304]{1,0:T(4,128)S(1)}, u32[]{:S(2)}, u32[]{:S(2)}) collective-permute-start(f32[4,2304]{1,0:T(4,128)S(1)} %get-tuple-element.29), channel_id=1, source_target_pairs={{0,0},{1,32},{2,2},{3,34},{4,4},{5,36},{6,6},{7,38},{8,8},{9,40},{... | collective-permute-start | bytes 110600 | tf_op jit(solution)/shard_map/ppermute | solution.py:33
  42.4 0.5 collective-permute-start.9
  42.9 3.0 %response.1 = bf16[1024,128]{1,0:T(8,128)(2,1)} custom-call(s32[4]{0:T(128)S(1)} %pad_add_fusion.place, bf16[27,128,128]{2,1,0:T(8,128)(2,1)S(1)} %copy-done, bf16[1024,128]{1,0:T(8,128)(2,1)S(1)} %collective-permute-done.near_vol.partner_plane, bf16[1024,128]{1,0:T(8,128)(2,1)S(1)} %bitcast.29, bf16[1024,128]{1,0:T(8,128)(2,1)S(1)} %collective-permute-done.2.other_plane), custom_call_target="tpu_custom_call" | custom-call | flops 1048576 | bytes 65536 | tf_op jit(solution)/shard_map/response/pallas_call | solution.py:221
  45.9 1.8 %collective-permute-done.9 = f32[4,2304]{1,0:T(4,128)S(1)} collective-permute-done((f32[4,2304]{1,0:T(4,128)S(1)}, f32[4,2304]{1,0:T(4,128)S(1)}, u32[]{:S(2)}, u32[]{:S(2)}) %collective-permute-start.9) | collective-permute-done | bytes 36896 | tf_op jit(solution)/shard_map/ppermute | solution.py:33
  47.7 1.4 %collective-permute-start.12 = (f32[4,2304]{1,0:T(4,128)S(1)}, f32[4,2304]{1,0:T(4,128)S(1)}, u32[]{:S(2)}, u32[]{:S(2)}) collective-permute-start(f32[4,2304]{1,0:T(4,128)S(1)} %add_add_fusion), channel_id=1, source_target_pairs={{0,64},{1,65},{2,66},{3,67},{4,68},{5,69},{6,70},{7,71},{8,72},{9,... | collective-permute-start | bytes 110600 | tf_op jit(solution)/shard_map/ppermute | solution.py:33
  49.1 1.5 %collective-permute-done.12 = f32[4,2304]{1,0:T(4,128)S(1)} collective-permute-done((f32[4,2304]{1,0:T(4,128)S(1)}, f32[4,2304]{1,0:T(4,128)S(1)}, u32[]{:S(2)}, u32[]{:S(2)}) %collective-permute-start.12) | collective-permute-done | bytes 36896 | tf_op jit(solution)/shard_map/ppermute | solution.py:33
  50.6 2.8 %collective-permute-start.13 = (f32[4,2304]{1,0:T(4,128)S(1)}, f32[4,2304]{1,0:T(4,128)S(1)}, u32[]{:S(2)}, u32[]{:S(2)}) collective-permute-start(f32[4,2304]{1,0:T(4,128)S(1)} %add.38), channel_id=1, source_target_pairs={{0,192},{1,193},{2,194},{3,195},{4,196},{5,197},{6,198},{7,199},{8... | collective-permute-start | bytes 110600 | tf_op jit(solution)/shard_map/ppermute | solution.py:33
  53.4 1.4 %collective-permute-done.13 = f32[4,2304]{1,0:T(4,128)S(1)} collective-permute-done((f32[4,2304]{1,0:T(4,128)S(1)}, f32[4,2304]{1,0:T(4,128)S(1)}, u32[]{:S(2)}, u32[]{:S(2)}) %collective-permute-start.13) | collective-permute-done | bytes 36896 | tf_op jit(solution)/shard_map/ppermute | solution.py:33
  54.9 0.5 collective-permute-start.14
  55.3 0.9 %collective-permute-done.14 = f32[4,2304]{1,0:T(4,128)S(1)} collective-permute-done((f32[4,2304]{1,0:T(4,128)S(1)}, f32[4,2304]{1,0:T(4,128)S(1)}, u32[]{:S(2)}, u32[]{:S(2)}) %collective-permute-start.14) | collective-permute-done | bytes 36896 | tf_op jit(solution)/shard_map/ppermute | solution.py:33
  56.3 0.6 %copy.7 = f32[4,3,3,3,128]{4,0,3,2,1:T(4,128)} copy(f32[4,3,3,3,128]{4,0,2,3,1:T(4,128)S(1)} %fusion.7) | data formatting | bytes 110592 | tf_op jit(solution)/shard_map/mul | solution.py:285
  (29 shorter events, 0.7 us)
Async XLA Ops:
  0.6 13.8 %collective-permute-start = (bf16[1024,128]{1,0:T(8,128)(2,1)}, bf16[1024,128]{1,0:T(8,128)(2,1)S(1)}, u32[]{:S(2)}, u32[]{:S(2)}) collective-permute-start(bf16[1024,128]{1,0:T(8,128)(2,1)} %bitcast.25), channel_id=1, source_target_pairs={{0,1},{1,0},{2,3},{3,2},{4,5},{5,4},{6,7},{7,6},{8,9},{9,8},{10,11... | collective-permute-start | bytes 786440 | tf_op jit(solution)/shard_map/ppermute | solution.py:33
  3.2 11.2 %collective-permute-start.1 = (bf16[1024,128]{1,0:T(8,128)(2,1)}, bf16[1024,128]{1,0:T(8,128)(2,1)S(1)}, u32[]{:S(2)}, u32[]{:S(2)}) collective-permute-start(bf16[1024,128]{1,0:T(8,128)(2,1)} %bitcast.30), channel_id=1, source_target_pairs={{1,2},{2,1},{3,4},{4,3},{5,6},{6,5},{7,8},{8,7},{9,10},{10,9},{11,... | collective-permute-start | bytes 786440 | tf_op jit(solution)/shard_map/ppermute | solution.py:33
  3.9 13.1 %collective-permute-start.2 = (bf16[1024,128]{1,0:T(8,128)(2,1)}, bf16[1024,128]{1,0:T(8,128)(2,1)S(1)}, u32[]{:S(2)}, u32[]{:S(2)}) collective-permute-start(bf16[1024,128]{1,0:T(8,128)(2,1)} %bitcast.26), channel_id=1, source_target_pairs={{1,2},{2,1},{3,4},{4,3},{5,6},{6,5},{7,8},{8,7},{9,10},{10,9},{11,... | collective-permute-start | bytes 786440 | tf_op jit(solution)/shard_map/ppermute | solution.py:33
  4.5 12.4 %collective-permute-start.3 = (bf16[1024,128]{1,0:T(8,128)(2,1)}, bf16[1024,128]{1,0:T(8,128)(2,1)S(1)}, u32[]{:S(2)}, u32[]{:S(2)}) collective-permute-start(bf16[1024,128]{1,0:T(8,128)(2,1)} %bitcast.31), channel_id=1, source_target_pairs={{0,1},{1,0},{2,3},{3,2},{4,5},{5,4},{6,7},{7,6},{8,9},{9,8},{10,11... | collective-permute-start | bytes 786440 | tf_op jit(solution)/shard_map/ppermute | solution.py:33
  10.5 1.0 %copy-start.1 = (bf16[1,1,32,32,128]{4,3,2,1,0:T(8,128)(2,1)S(1)}, bf16[1,1,32,32,128]{4,3,2,1,0:T(8,128)(2,1)}, u32[]{:S(2)}) copy-start(bf16[1,1,32,32,128]{4,3,2,1,0:T(8,128)(2,1)} %param.3) | copy-start | bytes 786436
  11.4 0.9 %copy-start.3 = (bf16[1,1,32,32,128]{4,3,2,1,0:T(8,128)(2,1)S(1)}, bf16[1,1,32,32,128]{4,3,2,1,0:T(8,128)(2,1)}, u32[]{:S(2)}) copy-start(bf16[1,1,32,32,128]{4,3,2,1,0:T(8,128)(2,1)} %param.5) | copy-start | bytes 786436
  12.4 2.1 %copy-start.2 = (bf16[1,1,32,32,128]{4,3,2,1,0:T(8,128)(2,1)S(1)}, bf16[1,1,32,32,128]{4,3,2,1,0:T(8,128)(2,1)}, u32[]{:S(2)}) copy-start(bf16[1,1,32,32,128]{4,3,2,1,0:T(8,128)(2,1)} %param.3) | copy-start | bytes 786436
  16.9 3.3 %collective-permute-start.4 = (f32[4,16,2304]{2,1,0:T(8,128)S(1)}, f32[4,16,2304]{2,1,0:T(8,128)S(1)}, u32[]{:S(2)}, u32[]{:S(2)}) collective-permute-start(f32[4,16,2304]{2,1,0:T(8,128)S(1)} %get-tuple-element.18), channel_id=1, source_target_pairs={{0,32},{1,33},{2,34},{3,35},{4,36},{5,37},{6,38},{7,39},{8,40},{9,... | collective-permute-start | bytes 1769480 | tf_op jit(solution)/shard_map/ppermute | solution.py:33
  20.3 8.2 %copy-start = (bf16[27,128,128]{2,1,0:T(8,128)(2,1)S(1)}, bf16[27,128,128]{2,1,0:T(8,128)(2,1)}, u32[]{:S(2)}) copy-start(bf16[27,128,128]{2,1,0:T(8,128)(2,1)} %weights.3) | copy-start | bytes 2654212
  20.7 10.8 %collective-permute-start.7 = (f16[16,2432]{1,0:T(8,128)(2,1)S(1)}, f16[16,2432]{1,0:T(8,128)(2,1)S(1)}, u32[]{:S(2)}, u32[]{:S(2)}) collective-permute-start(f16[16,2432]{1,0:T(8,128)(2,1)S(1)} %get-tuple-element.24), channel_id=1, source_target_pairs={{0,24},{1,25},{2,26},{3,27},{4,28},{5,29},{6,30},{7,31},{8,16},{9,... | collective-permute-start | bytes 233480 | tf_op jit(solution)/shard_map/ppermute | solution.py:33
  27.8 4.8 %collective-permute-start.6 = (f16[16,2432]{1,0:T(8,128)(2,1)S(1)}, f16[16,2432]{1,0:T(8,128)(2,1)S(1)}, u32[]{:S(2)}, u32[]{:S(2)}) collective-permute-start(f16[16,2432]{1,0:T(8,128)(2,1)S(1)} %get-tuple-element.25), channel_id=1, source_target_pairs={{0,16},{1,17},{2,18},{3,19},{4,20},{5,21},{6,22},{7,23},{8,24},{9,... | collective-permute-start | bytes 233480 | tf_op jit(solution)/shard_map/ppermute | solution.py:33
  28.0 4.6 %collective-permute-start.5 = (f16[16,2432]{1,0:T(8,128)(2,1)S(1)}, f16[16,2432]{1,0:T(8,128)(2,1)S(1)}, u32[]{:S(2)}, u32[]{:S(2)}) collective-permute-start(f16[16,2432]{1,0:T(8,128)(2,1)S(1)} %get-tuple-element.23), channel_id=1, source_target_pairs={{0,8},{1,9},{2,10},{3,11},{4,12},{5,13},{6,14},{7,15},{8,0},{9,1},... | collective-permute-start | bytes 233480 | tf_op jit(solution)/shard_map/ppermute | solution.py:33
  33.0 12.9 %collective-permute-start.10 = (f32[4,2304]{1,0:T(4,128)S(1)}, f32[4,2304]{1,0:T(4,128)S(1)}, u32[]{:S(2)}, u32[]{:S(2)}) collective-permute-start(f32[4,2304]{1,0:T(4,128)S(1)} %get-tuple-element.28), channel_id=1, source_target_pairs={{0,4},{1,36},{2,6},{3,38},{4,0},{5,32},{6,2},{7,34},{8,12},{9,44},... | collective-permute-start | bytes 110600 | tf_op jit(solution)/shard_map/ppermute | solution.py:33
  37.4 8.5 %collective-permute-start.11 = (f32[4,2304]{1,0:T(4,128)S(1)}, f32[4,2304]{1,0:T(4,128)S(1)}, u32[]{:S(2)}, u32[]{:S(2)}) collective-permute-start(f32[4,2304]{1,0:T(4,128)S(1)} %get-tuple-element.27), channel_id=1, source_target_pairs={{0,6},{1,38},{2,4},{3,36},{4,2},{5,34},{6,0},{7,32},{8,14},{9,46},... | collective-permute-start | bytes 110600 | tf_op jit(solution)/shard_map/ppermute | solution.py:33
  37.5 8.4 %collective-permute-start.8 = (f32[4,2304]{1,0:T(4,128)S(1)}, f32[4,2304]{1,0:T(4,128)S(1)}, u32[]{:S(2)}, u32[]{:S(2)}) collective-permute-start(f32[4,2304]{1,0:T(4,128)S(1)} %get-tuple-element.29), channel_id=1, source_target_pairs={{0,0},{1,32},{2,2},{3,34},{4,4},{5,36},{6,6},{7,38},{8,8},{9,40},{... | collective-permute-start | bytes 110600 | tf_op jit(solution)/shard_map/ppermute | solution.py:33
  42.4 5.3 %collective-permute-start.9 = (f32[4,2304]{1,0:T(4,128)S(1)}, f32[4,2304]{1,0:T(4,128)S(1)}, u32[]{:S(2)}, u32[]{:S(2)}) collective-permute-start(f32[4,2304]{1,0:T(4,128)S(1)} %get-tuple-element.26), channel_id=1, source_target_pairs={{0,2},{1,34},{2,0},{3,32},{4,6},{5,38},{6,4},{7,36},{8,10},{9,42},... | collective-permute-start | bytes 110600 | tf_op jit(solution)/shard_map/ppermute | solution.py:33
  47.7 2.9 %collective-permute-start.12 = (f32[4,2304]{1,0:T(4,128)S(1)}, f32[4,2304]{1,0:T(4,128)S(1)}, u32[]{:S(2)}, u32[]{:S(2)}) collective-permute-start(f32[4,2304]{1,0:T(4,128)S(1)} %add_add_fusion), channel_id=1, source_target_pairs={{0,64},{1,65},{2,66},{3,67},{4,68},{5,69},{6,70},{7,71},{8,72},{9,... | collective-permute-start | bytes 110600 | tf_op jit(solution)/shard_map/ppermute | solution.py:33
  50.6 4.3 %collective-permute-start.13 = (f32[4,2304]{1,0:T(4,128)S(1)}, f32[4,2304]{1,0:T(4,128)S(1)}, u32[]{:S(2)}, u32[]{:S(2)}) collective-permute-start(f32[4,2304]{1,0:T(4,128)S(1)} %add.38), channel_id=1, source_target_pairs={{0,192},{1,193},{2,194},{3,195},{4,196},{5,197},{6,198},{7,199},{8... | collective-permute-start | bytes 110600 | tf_op jit(solution)/shard_map/ppermute | solution.py:33
  54.9 1.3 %collective-permute-start.14 = (f32[4,2304]{1,0:T(4,128)S(1)}, f32[4,2304]{1,0:T(4,128)S(1)}, u32[]{:S(2)}, u32[]{:S(2)}) collective-permute-start(f32[4,2304]{1,0:T(4,128)S(1)} %add.39), channel_id=1, source_target_pairs={{0,32},{1,33},{2,34},{3,35},{4,36},{5,37},{6,38},{7,39},{8,40},{9,... | collective-permute-start | bytes 110600 | tf_op jit(solution)/shard_map/ppermute | solution.py:33
